TPU v7x, 32 devices: a whole 2x2x4 slice. The times are simulated.
32 devices in a mesh: mod: 2 (over x), dp: 16 (over z, y, core).
Axes of the slice: x: 2, y: 2, z: 4, core: 2. Of those that a mesh axis runs over, the one named last changes fastest.
Arguments:
- layer_rows: bfloat16 [2, 16384, 768], P('mod', 'dp'), may hold values from -6 to 6
- cotangent: bfloat16 [2, 16384, 768], P('mod', 'dp'), may hold values from -6 to 6
- row_live: int32 [2, 16384], P(None, 'dp'), may hold values from 0 to 1, as said below
- partner: int32 [16, 16], P('dp'), may hold values from 0 to 15, as said below
- w_qkv: bfloat16 [768, 2304], replicated, may hold values from -0.21875 to 0.21875
- b_qv: float32 [2, 768], replicated, may hold values from -1.8 to 1.8
- w_out: bfloat16 [768, 768], replicated, may hold values from -0.875 to 0.875
- norm_gains: float32 [2, 768], replicated, may hold values from 0.5 to 1.5
- bias_rows: float32 [4, 768], replicated, may hold values from -1.8 to 1.8
- w_in: bfloat16 [768, 3072], replicated, may hold values from -0.21875 to 0.21875
- b_in: float32 [3072], replicated, may hold values from -1.8 to 1.8
- w_back: bfloat16 [3072, 768], replicated, may hold values from -0.15625 to 0.15625
Outputs:
- output: bfloat16 [2, 16384, 768], P('mod', 'dp')
- grad_rows: bfloat16 [2, 16384, 768], P('mod', 'dp')
- grad_w_qkv: float32 [768, 2304], P('dp')
- grad_b_qv: float32 [2, 768], P(None, 'dp')
- grad_w_out: float32 [768, 768], P('dp')
- grad_gains: float32 [2, 768], P(None, 'dp')
- grad_biases: float32 [4, 768], P(None, 'dp')
- grad_w_in: float32 [768, 3072], P('dp')
- grad_b_in: float32 [3072], P('dp')
- grad_w_back: float32 [3072, 768], P('dp')
Inputs may be any that keep to these rules, and one draw needn't show every extreme that they name: `row_live`: within each pair and modality the live rows are the first ones of its 64 slots, at least one; the first pair of every index of dp is live in all its rows of both modalities. Each row partner[g] is a permutation of the 16 region slots of index g of dp.
All inputs are finite; a program needn't handle non-finite values.
Results may differ from a plain program's by a relative error of at most 0.015.
Values may be sent and summed in bfloat16 or wider, within the bound.
No kernel may reach another device: no remote copies, remote signals or barrier semaphores. Data moves between devices by JAX's collectives and lax.ppermute only.
A program may use at most 192 MiB of HBM per device.

v0:
```python
import jax
import jax.numpy as jnp
from jax import lax
from jax.sharding import PartitionSpec as P

HEADS = 12


EPSILON = 1e-12


def swapped(value, axis, apart):
    mask = 2**apart
    pairs = [(source, source ^ mask) for source in range(lax.axis_size(axis))]
    return lax.ppermute(value, axis, pairs)


def layer_norm(values_in, gain_row, bias_row):
    centered = values_in - jnp.mean(values_in, axis=-1, keepdims=True)
    spread = jnp.mean(centered * centered, axis=-1, keepdims=True)
    return centered * lax.rsqrt(spread + EPSILON) * gain_row + bias_row


def gelu_exact(values_in):
    return jax.nn.gelu(values_in, approximate=False)


def contract_rows(left_side, right_side):
    return lax.dot_general(
        left_side, right_side, (((0,), (0,)), ((), ())), preferred_element_type=jnp.float32
    )


def contract_cols(left_side, right_side):
    return lax.dot_general(
        left_side, right_side, (((1,), (1,)), ((), ())), preferred_element_type=jnp.float32
    )


def by_heads(values_in, groups):
    return values_in.reshape(groups, -1, HEADS, values_in.shape[-1] // HEADS)


def forward(local_rows, mine_live, far_live, fetch_far, weights):
    w_qkv, b_qv, w_out, norm_gains, bias_rows, w_in, b_in, w_back = weights
    groups, slot_rows, model_width = local_rows.shape
    score_scale = (model_width // HEADS) ** (-0.5)
    flat_rows = local_rows.reshape(groups * slot_rows, model_width)
    mixed_rows = jnp.dot(flat_rows, w_qkv, preferred_element_type=jnp.float32)
    queries = (mixed_rows[:, :model_width] + b_qv[0]).astype(jnp.bfloat16)
    own_keys = mixed_rows[:, model_width : 2 * model_width].astype(jnp.bfloat16)
    own_values = (mixed_rows[:, 2 * model_width :] + b_qv[1]).astype(jnp.bfloat16)
    own_pair = jnp.stack(
        [
            own_keys.reshape(groups, slot_rows, model_width),
            own_values.reshape(groups, slot_rows, model_width),
        ]
    )
    far_pair = fetch_far(own_pair)
    all_keys = by_heads(jnp.concatenate([own_pair[0], far_pair[0]], 1), groups)
    all_values = by_heads(jnp.concatenate([own_pair[1], far_pair[1]], 1), groups)
    head_queries = by_heads(queries, groups)
    seen_keys = jnp.concatenate([mine_live, far_live], 1)
    scores = (
        jnp.einsum("pqhe,pkhe->phqk", head_queries, all_keys, preferred_element_type=jnp.float32)
        * score_scale
    )
    scores = jnp.where(seen_keys[:, None, None, :], scores, -1e30)
    largest = jnp.max(scores, axis=-1, keepdims=True)
    powered = jnp.exp(scores - largest)
    softmaxed = powered / jnp.sum(powered, axis=-1, keepdims=True)
    low_probs = softmaxed.astype(jnp.bfloat16)
    context = jnp.einsum(
        "phqk,pkhe->pqhe", low_probs, all_values, preferred_element_type=jnp.float32
    )
    context = context.reshape(groups * slot_rows, model_width).astype(jnp.bfloat16)
    pre_one = (
        flat_rows.astype(jnp.float32)
        + jnp.dot(context, w_out, preferred_element_type=jnp.float32)
        + bias_rows[0]
    )
    hidden = layer_norm(pre_one, norm_gains[0], bias_rows[1])
    low_hidden = hidden.astype(jnp.bfloat16)
    inner_pre = jnp.dot(low_hidden, w_in, preferred_element_type=jnp.float32) + b_in
    low_act = gelu_exact(inner_pre).astype(jnp.bfloat16)
    pre_two = hidden + jnp.dot(low_act, w_back, preferred_element_type=jnp.float32) + bias_rows[2]
    result = layer_norm(pre_two, norm_gains[1], bias_rows[3])
    return {
        "flat_rows": flat_rows,
        "all_keys": all_keys,
        "all_values": all_values,
        "head_queries": head_queries,
        "softmaxed": softmaxed,
        "low_probs": low_probs,
        "context": context,
        "pre_one": pre_one,
        "low_hidden": low_hidden,
        "inner_pre": inner_pre,
        "low_act": low_act,
        "pre_two": pre_two,
        "result": result,
    }


def backward(kept_state, local_cot, give_back, weights):
    w_qkv, b_qv, w_out, norm_gains, bias_rows, w_in, b_in, w_back = weights
    groups, slot_rows, model_width = local_cot.shape
    score_scale = (model_width // HEADS) ** (-0.5)
    d_out = local_cot.reshape(groups * slot_rows, model_width).astype(jnp.float32)
    unused_two, norm_two_back = jax.vjp(
        layer_norm, kept_state["pre_two"], norm_gains[1], bias_rows[3]
    )
    d_pre_two, d_gain_two, d_bias_two = norm_two_back(d_out)
    low_branch = d_pre_two.astype(jnp.bfloat16)
    grad_w_back = contract_rows(kept_state["low_act"], low_branch)
    d_act = contract_cols(low_branch, w_back)
    unused_gelu, gelu_back = jax.vjp(gelu_exact, kept_state["inner_pre"])
    d_inner = gelu_back(d_act)[0]
    low_inner = d_inner.astype(jnp.bfloat16)
    grad_w_in = contract_rows(kept_state["low_hidden"], low_inner)
    d_hidden = d_pre_two + contract_cols(low_inner, w_in)
    unused_one, norm_one_back = jax.vjp(
        layer_norm, kept_state["pre_one"], norm_gains[0], bias_rows[1]
    )
    d_pre_one, d_gain_one, d_bias_one = norm_one_back(d_hidden)
    low_attn = d_pre_one.astype(jnp.bfloat16)
    grad_w_out = contract_rows(kept_state["context"], low_attn)
    d_context = by_heads(contract_cols(low_attn, w_out).astype(jnp.bfloat16), groups)
    all_values = kept_state["all_values"]
    softmaxed = kept_state["softmaxed"]
    d_probs = jnp.einsum(
        "pqhe,pkhe->phqk", d_context, all_values, preferred_element_type=jnp.float32
    )
    d_all_values = jnp.einsum(
        "phqk,pqhe->pkhe", kept_state["low_probs"], d_context, preferred_element_type=jnp.float32
    )
    d_scores = softmaxed * (d_probs - jnp.sum(softmaxed * d_probs, axis=-1, keepdims=True))
    d_scores = d_scores.astype(jnp.bfloat16)
    d_queries = (
        jnp.einsum(
            "phqk,pkhe->pqhe", d_scores, kept_state["all_keys"], preferred_element_type=jnp.float32
        )
        * score_scale
    )
    d_all_keys = (
        jnp.einsum(
            "phqk,pqhe->pkhe",
            d_scores,
            kept_state["head_queries"],
            preferred_element_type=jnp.float32,
        )
        * score_scale
    )
    cross_pair = jnp.stack([d_all_keys[:, slot_rows:], d_all_values[:, slot_rows:]]).astype(
        jnp.bfloat16
    )
    returned = give_back(cross_pair).astype(jnp.float32)
    d_keys = (d_all_keys[:, :slot_rows] + returned[0]).astype(jnp.bfloat16).reshape(-1, model_width)
    d_values = (
        (d_all_values[:, :slot_rows] + returned[1]).astype(jnp.bfloat16).reshape(-1, model_width)
    )
    low_queries = d_queries.astype(jnp.bfloat16).reshape(-1, model_width)
    d_mixed = jnp.concatenate([low_queries, d_keys, d_values], 1)
    grad_w_qkv = contract_rows(kept_state["flat_rows"], d_mixed)
    d_rows = d_pre_one + contract_cols(d_mixed, w_qkv)
    grad_b_qv = jnp.stack(
        [
            jnp.sum(low_queries.astype(jnp.float32), axis=0),
            jnp.sum(d_values.astype(jnp.float32), axis=0),
        ]
    )
    grad_gains = jnp.stack([d_gain_one, d_gain_two])
    grad_biases = jnp.stack(
        [jnp.sum(d_pre_one, axis=0), d_bias_one, jnp.sum(d_pre_two, axis=0), d_bias_two]
    )
    grad_b_in = jnp.sum(d_inner, axis=0)
    grads = (
        grad_w_qkv,
        grad_b_qv,
        grad_w_out,
        grad_gains,
        grad_biases,
        grad_w_in,
        grad_b_in,
        grad_w_back,
    )
    return (d_rows.astype(jnp.bfloat16).reshape(groups, slot_rows, model_width), grads)


def run_layer(local_rows, local_cot, mine_live, far_live, fetch_far, give_back, weights):
    kept_state = forward(local_rows, mine_live, far_live, fetch_far, weights)
    output = kept_state["result"].astype(jnp.bfloat16).reshape(local_rows.shape)
    kept_state = forward(local_rows, mine_live, far_live, fetch_far, weights)
    d_rows, grads = backward(kept_state, local_cot, give_back, weights)
    return (output, d_rows, grads)


def body(
    layer_rows,
    cotangent,
    row_live,
    partner,
    w_qkv,
    b_qv,
    w_out,
    norm_gains,
    bias_rows,
    w_in,
    b_in,
    w_back,
):
    weights = (w_qkv, b_qv, w_out, norm_gains, bias_rows, w_in, b_in, w_back)
    side_index = lax.axis_index("mod")
    is_first = side_index == 0
    groups = partner.shape[1]
    model_width = layer_rows.shape[2]
    slot_rows = layer_rows.shape[1] // groups
    own_rows = layer_rows[0].reshape(groups, slot_rows, model_width)
    own_cot = cotangent[0].reshape(groups, slot_rows, model_width)
    words_live = row_live[0].reshape(groups, slot_rows) > 0
    region_live = row_live[1].reshape(groups, slot_rows) > 0
    partner_slot = partner[0]
    counting = jnp.arange(groups, dtype=jnp.int32)
    inverse = jnp.zeros((groups,), jnp.int32).at[partner_slot].set(counting)
    fore_index = jnp.where(is_first, partner_slot, inverse)
    back_index = jnp.where(is_first, inverse, partner_slot)
    mine_live = jnp.where(is_first, words_live, region_live)
    far_live = jnp.where(is_first, region_live, words_live)[fore_index]

    def fetch_far(stacked):
        return swapped(stacked, "mod", 0)[:, fore_index]

    def give_back(stacked):
        return swapped(stacked[:, back_index], "mod", 0)

    output, d_rows, grads = run_layer(
        own_rows, own_cot, mine_live, far_live, fetch_far, give_back, weights
    )
    placed = jnp.stack([output, d_rows])
    summed = (
        lax.psum_scatter(grads[0], "dp", scatter_dimension=0, tiled=True),
        lax.psum_scatter(grads[1], "dp", scatter_dimension=1, tiled=True),
        lax.psum_scatter(grads[2], "dp", scatter_dimension=0, tiled=True),
        lax.psum_scatter(grads[3], "dp", scatter_dimension=1, tiled=True),
        lax.psum_scatter(grads[4], "dp", scatter_dimension=1, tiled=True),
        lax.psum_scatter(grads[5], "dp", scatter_dimension=0, tiled=True),
        lax.psum_scatter(grads[6], "dp", scatter_dimension=0, tiled=True),
        lax.psum_scatter(grads[7], "dp", scatter_dimension=0, tiled=True),
    )
    summed = (
        lax.psum(summed[0].astype(jnp.bfloat16), "mod").astype(jnp.float32),
        lax.psum(summed[1].astype(jnp.bfloat16), "mod").astype(jnp.float32),
        lax.psum(summed[2].astype(jnp.bfloat16), "mod").astype(jnp.float32),
        lax.psum(summed[3].astype(jnp.bfloat16), "mod").astype(jnp.float32),
        lax.psum(summed[4].astype(jnp.bfloat16), "mod").astype(jnp.float32),
        lax.psum(summed[5].astype(jnp.bfloat16), "mod").astype(jnp.float32),
        lax.psum(summed[6].astype(jnp.bfloat16), "mod").astype(jnp.float32),
        lax.psum(summed[7].astype(jnp.bfloat16), "mod").astype(jnp.float32),
    )
    out_rows = placed[0].reshape(1, groups * slot_rows, model_width)
    grad_local = placed[1].reshape(1, groups * slot_rows, model_width)
    return (
        out_rows,
        grad_local,
        summed[0],
        summed[1],
        summed[2],
        summed[3],
        summed[4],
        summed[5],
        summed[6],
        summed[7],
    )


def solution(mesh):
    placed = (
        P("mod", "dp", None),
        P("mod", "dp", None),
        P(None, "dp"),
        P("dp", None),
        P(),
        P(),
        P(),
        P(),
        P(),
        P(),
        P(),
        P(),
    )
    return jax.shard_map(
        body,
        mesh=mesh,
        in_specs=placed,
        out_specs=(
            P("mod", "dp", None),
            P("mod", "dp", None),
            P("dp", None),
            P(None, "dp"),
            P("dp", None),
            P(None, "dp"),
            P(None, "dp"),
            P("dp", None),
            P("dp"),
            P("dp", None),
        ),
        check_vma=False,
    )
```

profile of v0, /device:TPU:0, one launch (start us, length us, event | category | flops | bytes accessed | tf_op | source)
XLA Modules:
  0.0 913.9 jit_solution(11217170056336145765)
XLA Ops:
  9.2 5.2 fusion.35
  24.1 5.9 reshape.209
  30.0 5.9 reshape.210
  40.0 5.9 reshape.230
  45.9 6.5 copy.75
  52.4 6.5 copy.63
  58.9 6.5 copy.67
  72.8 17.2 %collective-permute-done = bf16[2,16,64,768]{3,2,1,0:T(8,128)(2,1)} collective-permute-done((bf16[2,16,64,768]{3,2,1,0:T(8,128)(2,1)}, bf16[2,16,64,768]{3,2,1,0:T(8,128)(2,1)}, u32[]{:S(2)}, u32[]{:S(2)}) %collective-permute-start) | collective-permute-done | bytes 3145760 | tf_op jit(solution)/shard_map/ppermute | solution.py:15
  89.9 4.3 gather_fusion
  98.1 4.1 copy.66
  102.2 4.2 copy.62
  106.4 6.1 fusion.42
  112.6 4.9 fusion.63
  121.3 4.1 copy.69
  125.5 5.4 convert_element_type.141
  135.8 35.9 %multiply_convert_fusion = (bf16[1024,3072]{1,0:T(8,128)(2,1)}, f32[1024,3072]{1,0:T(8,128)}, f32[1024,3072]{1,0:T(8,128)}) fusion(f32[3072]{0:T(1024)S(1)} %copy-done.41, bf16[768,3072]{1,0:T(8,128)(2,1)S(1)} %bitcast.133, f32[1024,768]{0,1:T(8,128)S(1)} %get-tuple-element.82, f32[768]{0:T(1024)S(1)} %copy-done.35, f32[768]{0:T(1024)S(1)} %get-tuple-element.93, ...), kind=kOutput, calls=%fused_computation.8 | convolution fusion | flops 5043388416 | bytes 39348224 | tf_op jit(solution)/shard_map/dot_general | solution.py:84
  171.7 7.8 fusion.65
  186.1 19.6 %fusion.66 = (f32[3072]{0:T(1024)}, bf16[1024,3072]{1,0:T(8,128)(2,1)}) fusion(f32[1024,3072]{1,0:T(8,128)} %get-tuple-element.70, bf16[3072,768]{1,0:T(8,128)(2,1)} %param.23, f32[1024,768]{0,1:T(8,128)} %get-tuple-element.68, f32[1024]{0:T(1024)S(1)} %negate_multiply_fusion.2, f32[1024,3072]{1,0:T(8,128)} %get-tuple-element.83, f32[3072]{0:T(1024)S(1)} %copy-done.41), kind=kOutput, calls=%fused_computation.150 | convolution fusion | flops 4883739648 | bytes 39350272 | tf_op jit(solution)/shard_map/dot_general | solution.py:35
  205.7 12.2 %multiply_reduce_fusion.1 = (f32[768]{0:T(1024)}, f32[1024]{0:T(1024)S(1)}, f32[768]{0:T(1024)}, f32[1024,768]{0,1:T(8,128)S(1)}) fusion(f32[1024,768]{0,1:T(8,128)} %copy-done.10, f32[1024]{0:T(1024)S(1)} %fusion.44, f32[1024]{0:T(1024)S(1)} %broadcast_multiply_fusion.1, f32[768]{0:T(1024)S(1)} %copy-done.28, bf16[768,3072]{1,0:T(8,128)(2,1)} %param.21, ...), kind=kOutput, calls=%fused_computation.62 | convolution fusion | flops 4839699456 | bytes 20472832 | tf_op jit(solution)/shard_map/dot_general | solution.py:35
  223.0 5.9 reshape.231
  228.9 6.5 copy.76
  235.4 9.7 %multiply_reduce_fusion = (f32[16,12,64]{2,1,0:T(8,128)S(1)}, f32[16,12,64,128]{3,2,1,0:T(8,128)S(1)}) fusion(f32[16,12,64,128]{3,2,1,0:T(8,128)} %copy-done.13, f32[16,12,64]{2,1,0:T(8,128)} %copy-done.18, bf16[16,64,12,64]{1,3,2,0:T(8,128)(2,1)} %copy.76, bf16[16,64,12,64]{1,3,2,0:T(8,128)(2,1)} %bitcast.122, bf16[16,64,12,64]{1,3,2,0:T(8,128)(2,1)} %copy.63), kind=kOutput, calls=%fused_computation.36 | convolution fusion | flops 212324352 | bytes 17399808 | tf_op jit(solution)/shard_map/pqhe,pkhe->phqk/dot_general | solution.py:131
  245.2 4.8 convolution_bitcast_fusion.1
  250.0 9.3 %multiply_convert_fusion.2 = bf16[16,12,64,128]{3,2,1,0:T(8,128)(2,1)S(1)} fusion(f32[16,12,64,128]{3,2,1,0:T(8,128)S(1)} %get-tuple-element.88, f32[16,12,64]{2,1,0:T(8,128)S(1)} %get-tuple-element.87, f32[16,12,64,128]{3,2,1,0:T(8,128)} %copy-done.13, f32[16,12,64]{2,1,0:T(8,128)S(1)} %copy-done.19), kind=kLoop, calls=%fused_computation.35 | loop fusion | flops 6291456 | bytes 15826944 | tf_op jit(solution)/shard_map/convert_element_type | solution.py:138
  265.6 4.1 pad_maximum_fusion
  269.7 6.9 gather_fusion.2
  287.7 5.2 fusion.41
  293.0 9.2 %convert_reduce_fusion.1 = (f32[12,64]{1,0:T(8,128)}, bf16[16,64,12,64]{3,1,2,0:T(8,128)(2,1)}) fusion(bf16[16,12,64,128]{3,2,1,0:T(8,128)(2,1)} %copy-done.3, bf16[16,64,12,64]{1,3,2,0:T(8,128)(2,1)} %bitcast.117, bf16[16,64,12,64]{1,3,2,0:T(8,128)(2,1)} %copy.67), kind=kOutput, calls=%fused_computation.32 | convolution fusion | flops 210763008 | bytes 7867392 | tf_op jit(solution)/shard_map/phqk,pkhe->pqhe/dot_general | solution.py:140
  302.1 5.5 copy.74
  307.6 5.4 reshape.167
  315.7 98.0 %collective-permute-done.1 = bf16[2,16,64,12,64]{2,4,3,0,1:T(8,128)(2,1)} collective-permute-done((bf16[2,16,64,12,64]{2,4,3,0,1:T(8,128)(2,1)}, bf16[2,16,64,12,64]{2,4,3,0,1:T(8,128)(2,1)}, u32[]{:S(2)}, u32[]{:S(2)}) %collective-permute-start.1) | collective-permute-done | bytes 3145760 | tf_op jit(solution)/shard_map/ppermute | solution.py:15
  413.7 4.5 convert_element_type.154
  418.2 7.6 convert_reduce_fusion
  425.9 4.2 copy.78
  430.1 5.4 reshape.169
  435.5 6.1 copy.77
  441.6 5.4 reshape.168
  451.2 8.3 convolution_bitcast_fusion
  459.5 8.1 copy.89
  468.2 10.3 %fusion.40 = f32[3072,768]{1,0:T(8,128)} fusion(bf16[1024,3072]{1,0:T(8,128)(2,1)} %get-tuple-element.69, f32[1024,768]{0,1:T(8,128)} %get-tuple-element.68, f32[1024]{0:T(1024)S(1)} %copy-done.26), kind=kOutput, calls=%fused_computation.95 | convolution fusion | flops 4833411072 | bytes 18878464 | tf_op jit(solution)/shard_map/dot_general | solution.py:29
  479.2 11.0 %fusion.23 = f32[768,3072]{1,0:T(8,128)} fusion(bf16[1024,3072]{1,0:T(8,128)(2,1)} %get-tuple-element.92, f32[1024,768]{0,1:T(8,128)} %copy-done.10, f32[768]{0:T(1024)} %get-tuple-element.46, f32[768]{0:T(1024)} %copy-done.27, f32[1024]{0:T(1024)S(1)} %copy-done.24, f32[1024]{0:T(1024)S(1)} %broadcast_multiply_fusion.1), kind=kOutput, calls=%fused_computation.65 | convolution fusion | flops 4835770368 | bytes 18888704 | tf_op jit(solution)/shard_map/dot_general | solution.py:29
  497.8 62.2 %all-reduce = bf16[3072]{0:T(1024)(128)(2,1)} all-reduce(f32[3072]{0:T(1024)S(1)} %copy-done.31), channel_id=8, replica_groups=mesh['mod'=2,'dp'=16] {'dp'}, use_global_device_ids=true, to_apply=%region_33.34.clone | all-reduce | flops 3072 | bytes 18432
  566.6 109.8 %reduce-scatter.20.cloned.1.call-done = f32[192,768]{1,0:T(8,128)} async-done(((f32[3072,768]{1,0:T(8,128)}), f32[192,768]{1,0:T(8,128)}) %reduce-scatter.20.cloned.1.call-update) | async-done | bytes 589840 | tf_op jit(solution)/shard_map/reduce_scatter | solution.py:248
  678.2 113.9 %reduce-scatter.18.cloned.1.call-done = f32[48,3072]{1,0:T(8,128)} async-done(((f32[768,3072]{1,0:T(8,128)}), f32[48,3072]{1,0:T(8,128)}) %reduce-scatter.18.cloned.1.call-update) | async-done | bytes 589840 | tf_op jit(solution)/shard_map/reduce_scatter | solution.py:246
  793.9 7.8 fusion.39
  804.3 47.2 %reduce-scatter.24.cloned.1.call-done = f32[48,2]{1,0:T(8,128)} async-done(((f32[768,2]{1,0:T(8,128)}), f32[48,2]{1,0:T(8,128)}) %reduce-scatter.24.cloned.1.call-update) | async-done | bytes 400
  852.3 5.6 all-reduce.1
  862.1 37.2 %all-reduce.5.cloned.1.call-done = (bf16[48,2304]{0,1:T(8,128)(2,1)}, bf16[48,768]{1,0:T(8,128)(2,1)}, bf16[48,3072]{1,0:T(8,128)(2,1)}, bf16[192,768]{1,0:T(8,128)(2,1)}) async-done(((bf16[48,2304]{0,1:T(8,128)(2,1)}, bf16[48,768]{1,0:T(8,128)(2,1)}, bf16[48,3072]{1,0:T(8,128)(2,1)}, bf16[192,768]{1,0:T(8,128)(2,1)}), (bf16[48,2304]{0,1:T(8,128)(2,1)}, bf16[48,768]{1,0:T(8,128)(2,1)}, ...) | async-done | bytes 884752 | tf_op jit(solution)/shard_map/psum | solution.py:251
  (193 shorter events, 104.7 us)
Async XLA Ops:
  7.2 2.0 copy-start
  7.2 554.1 %reduce-scatter.26.cloned.1.call-start = ((), (), s32[]{:S(2)}) async-start(), calls=%async_computation.12 | async-start | bytes 417792
  14.6 1.8 copy-start.6
  16.4 2.2 copy-start.7
  18.6 71.4 %collective-permute-start = (bf16[2,16,64,768]{3,2,1,0:T(8,128)(2,1)}, bf16[2,16,64,768]{3,2,1,0:T(8,128)(2,1)}, u32[]{:S(2)}, u32[]{:S(2)}) collective-permute-start(bf16[2,16,64,768]{3,2,1,0:T(8,128)(2,1)} %pad_maximum_fusion.1), channel_id=1, source_target_pairs={{0,16},{16,0},{1,17},{17,1},{2,18},{18,2},{3,19},{19,3},{4,20},{20... | collective-permute-start | bytes 9437192 | tf_op jit(solution)/shard_map/ppermute | solution.py:15
  30.0 5.9 copy-start.32
  58.9 6.5 copy-start.39
  72.8 98.9 %copy-start.27 = (f32[768]{0:T(1024)}, f32[768]{0:T(1024)S(1)}, u32[]{:S(2)}) copy-start(f32[768]{0:T(1024)S(1)} %get-tuple-element.93) | copy-start | bytes 9220
  106.4 6.1 copy-start.38
  112.6 5.0 copy-start.14
  112.6 5.0 copy-start.16
  117.5 3.8 copy-start.13
  117.5 3.8 copy-start.18
  125.5 5.4 copy-start.37
  130.9 4.5 slice-start.2
  130.9 4.5 slice-start.3
  130.9 40.8 %slice-start = ((s8[4718592]{0:T(1024)(128)(4,1)}), s8[4194304]{0:T(1024)(128)(4,1)S(1)}, s32[]{:S(2)}) async-start(s8[4718592]{0:T(1024)(128)(4,1)} %bitcast.130), calls=%async_computation.15 | async-start | bytes 8388608
  135.0 36.7 %copy-start.10 = (f32[1024,768]{0,1:T(8,128)}, f32[1024,768]{0,1:T(8,128)S(1)}, u32[]{:S(2)}) copy-start(f32[1024,768]{0,1:T(8,128)S(1)} %get-tuple-element.82) | copy-start | bytes 9437188
  135.4 82.5 %copy-start.23 = (f32[1024]{0:T(1024)}, f32[1024]{0:T(1024)S(1)}, u32[]{:S(2)}) copy-start(f32[1024]{0:T(1024)S(1)} %fusion.44) | copy-start | bytes 12292
  135.8 35.9 %copy-start.36 = (f32[768]{0:T(1024)S(1)}, f32[768]{0:T(1024)}, u32[]{:S(2)}) copy-start(f32[768]{0:T(1024)} %get-tuple-element.48) | copy-start | bytes 9220
  135.8 35.9 %slice-start.1 = ((s8[4718592]{0:T(1024)(128)(4,1)}), s8[524288]{0:T(1024)(128)(4,1)S(1)}, s32[]{:S(2)}) async-start(s8[4718592]{0:T(1024)(128)(4,1)} %bitcast.130), calls=%async_computation.16 | async-start | bytes 1048576
  180.0 2.9 copy-start.29
  186.1 94.6 %copy-start.25 = (f32[1024]{0:T(1024)}, f32[1024]{0:T(1024)S(1)}, u32[]{:S(2)}) copy-start(f32[1024]{0:T(1024)S(1)} %negate_multiply_fusion.2) | copy-start | bytes 12292
  186.1 19.6 %copy-start.28 = (f32[768]{0:T(1024)S(1)}, f32[768]{0:T(1024)}, u32[]{:S(2)}) copy-start(f32[768]{0:T(1024)} %copy-done.27) | copy-start | bytes 9220
  205.7 12.2 %copy-start.11 = (f32[1024,768]{0,1:T(8,128)S(1)}, f32[1024,768]{0,1:T(8,128)}, u32[]{:S(2)}) copy-start(f32[1024,768]{0,1:T(8,128)} %copy-done.10) | copy-start | bytes 9437188
  217.9 2.5 copy-start.40
  218.7 65.3 %copy-start.21 = (f32[1024]{0:T(1024)}, f32[1024]{0:T(1024)S(1)}, u32[]{:S(2)}) copy-start(f32[1024]{0:T(1024)S(1)} %negate_multiply_fusion.1) | copy-start | bytes 12292
  235.4 9.7 %copy-start.15 = (bf16[16,64,12,64]{1,3,2,0:T(8,128)(2,1)S(1)}, bf16[16,64,12,64]{1,3,2,0:T(8,128)(2,1)}, u32[]{:S(2)}) copy-start(bf16[16,64,12,64]{1,3,2,0:T(8,128)(2,1)} %copy.76) | copy-start | bytes 4718596
  235.4 9.8 %copy-start.19 = (f32[16,12,64]{2,1,0:T(8,128)S(1)}, f32[16,12,64]{2,1,0:T(8,128)}, u32[]{:S(2)}) copy-start(f32[16,12,64]{2,1,0:T(8,128)} %copy-done.18) | copy-start | bytes 147460
  250.0 12.9 %copy-start.5 = (f32[16,128,12,64]{1,3,2,0:T(8,128)}, f32[16,128,12,64]{1,3,2,0:T(8,128)S(1)}, u32[]{:S(2)}) copy-start(f32[16,128,12,64]{1,3,2,0:T(8,128)S(1)} %convolution_bitcast_fusion.1) | copy-start | bytes 18874372
  250.0 10.9 %copy-start.2 = (bf16[16,64,12,64]{1,3,2,0:T(8,128)(2,1)S(1)}, bf16[16,64,12,64]{1,3,2,0:T(8,128)(2,1)}, u32[]{:S(2)}) copy-start(bf16[16,64,12,64]{1,3,2,0:T(8,128)(2,1)} %copy.75) | copy-start | bytes 4718596
  261.9 2.7 copy-start.1
  269.7 11.0 %copy-start.30 = (f32[768]{0:T(1024)S(1)}, f32[768]{0:T(1024)}, u32[]{:S(2)}) copy-start(f32[768]{0:T(1024)} %get-tuple-element.42) | copy-start | bytes 9220
  276.7 6.8 copy-start.34
  276.7 6.8 copy-start.33
  276.7 7.4 copy-start.9
  276.7 137.0 %collective-permute-start.1 = (bf16[2,16,64,12,64]{2,4,3,0,1:T(8,128)(2,1)}, bf16[2,16,64,12,64]{2,4,3,0,1:T(8,128)(2,1)}, u32[]{:S(2)}, u32[]{:S(2)}) collective-permute-start(bf16[2,16,64,12,64]{2,4,3,0,1:T(8,128)(2,1)} %bitcast.121), channel_id=1, source_target_pairs={{0,16},{16,0},{1,17},{17,1},{2,18},{18,2},{3,19},{19,3},{4,20},{20... | collective-permute-start | bytes 9437192 | tf_op jit(solution)/shard_map/ppermute | solution.py:15
  285.9 276.2 %reduce-scatter.28.cloned.1.call-start = ((), (), s32[]{:S(2)}) async-start(), calls=%async_computation.13 | async-start | bytes 417792
  287.7 275.3 %reduce-scatter.16.cloned.1.call-start = ((), (), s32[]{:S(2)}) async-start(), calls=%async_computation.7 | async-start | bytes 2506752 | tf_op jit(solution)/shard_map/reduce_scatter | solution.py:243
  292.9 271.6 %reduce-scatter.22.cloned.1.call-start = ((), (), s32[]{:S(2)}) async-start(), calls=%async_computation.10 | async-start | bytes 7520256
  447.0 2.9 copy-start.12
  447.0 4.2 copy-start.17
  467.6 208.8 %reduce-scatter.20.cloned.1.call-start = ((), (), s32[]{:S(2)}) async-start(), calls=%async_computation.9 | async-start | bytes 10027008 | tf_op jit(solution)/shard_map/reduce_scatter | solution.py:248
  478.5 313.5 %reduce-scatter.18.cloned.1.call-start = ((), (), s32[]{:S(2)}) async-start(), calls=%async_computation.8 | async-start | bytes 10027008 | tf_op jit(solution)/shard_map/reduce_scatter | solution.py:246
  490.2 361.3 %reduce-scatter.24.cloned.1.call-start = ((), (), s32[]{:S(2)}) async-start(), calls=%async_computation.11 | async-start | bytes 417792
  493.3 4.6 copy-start.31
  493.3 406.1 %all-reduce.5.cloned.1.call-start = ((), (), s32[]{:S(2)}) async-start(), calls=%async_computation.14 | async-start | bytes 2506752 | tf_op jit(solution)/shard_map/psum | solution.py:251
  495.2 298.7 %copy-start.22 = (f32[1024]{0:T(1024)S(1)}, f32[1024]{0:T(1024)}, u32[]{:S(2)}) copy-start(f32[1024]{0:T(1024)} %copy-done.21) | copy-start | bytes 12292
  (8 other events, 8.2 us)
Sparse Core Ops, SparseCore 0:
  286.0 56.1 reduce-scatter.25
  346.7 54.6 reduce-scatter.27
  405.2 61.9 reduce-scatter.15
  471.6 89.8 reduce-scatter.21
  565.4 110.9 reduce-scatter.19
  680.9 111.1 reduce-scatter.17
  796.1 55.3 reduce-scatter.23
  855.3 44.0 all-reduce.4
where the time goes:
time: 923 us; the launch traced here: 914 us
  waiting for transfers between devices  423 us (46%)
  local copies, waits for them, and re-layouts  172 us (19%)
  matrix products  165 us (18%)
  blocking collectives  67.8 us (7%)
  other arithmetic  64.9 us (7%)
  between operations  15.8 us (2%)
    ppermute x2, waiting for transfers between devices, swapped(): return lax.ppermute(value, axis, pairs)  115 us
    reduce_scatter x1, waiting for transfers between devices, body(): lax.psum_scatter(grads[5], 'dp', scatter_dimension=0, tiled=True)  114 us
    reduce_scatter x1, waiting for transfers between devices, body(): lax.psum_scatter(grads[7], 'dp', scatter_dimension=0, tiled=True)  110 us
    unnamed x1, blocking collectives  62.2 us
    unnamed x12, waiting for transfers between devices  47.4 us
    unnamed x109, local copies, waits for them, and re-layouts  45.3 us
    dot_general x4, matrix products, contract_cols(): lax.dot_general(left_side, right_side, (((1,), (1,)), ((), ())), preferre...  42.2 us
    psum x1, waiting for transfers between devices, body(): lax.psum(summed[0].astype(jnp.bfloat16), 'mod').astype(jnp.float32)  37.2 us
  transfers between devices with their start and end apart: 10, of which 6 were waited for; matrix products, arithmetic and copies ran while one was open for 21% of the time, Pallas kernels for 0%

commit v1 on v0

v1 whole, which is shorter than its diff:
```python
import functools

import jax
import jax.numpy as jnp
from jax import lax
from jax.experimental import pallas as pl
from jax.experimental.pallas import tpu as pltpu
from jax.sharding import PartitionSpec as P

HEADS = 12
EPSILON = 1e-12
F32 = jnp.float32
BF16 = jnp.bfloat16
VMEM_LIMIT = 56 * 2**20


def dot(left, right, left_dim=1, right_dim=0):
    return lax.dot_general(
        left, right, (((left_dim,), (right_dim,)), ((), ())), preferred_element_type=F32
    )


def flipped(value, axis, mask):
    pairs = [(source, source ^ mask) for source in range(lax.axis_size(axis))]
    return lax.ppermute(value, axis, pairs)


def params(limit=VMEM_LIMIT):
    return pltpu.CompilerParams(vmem_limit_bytes=limit)


def kept_slot(scalars, pair, half):
    groups = 2 * half
    side = scalars[groups]
    place = side * half + pair
    return jnp.where(side == 0, place, scalars[place])


def sent_slot(scalars, pair, half):
    groups = 2 * half
    side = scalars[groups]
    place = (1 - side) * half + pair
    return jnp.where(side == 0, place, scalars[place])


def gather_sent(scalars, rows, half, cuts):
    slot_rows, width = rows.shape[1:]
    sizes = [cuts[i + 1] - cuts[i] for i in range(len(cuts) - 1)]

    def kernel(scalars_ref, rows_ref, *rest):
        outs, sems = rest[:-1], rest[-1]
        copies = []
        for part, out in enumerate(outs):
            for i in range(sizes[part]):
                pair = cuts[part] + i
                copies.append(
                    pltpu.make_async_copy(
                        rows_ref.at[sent_slot(scalars_ref, pair, half)], out.at[i], sems.at[pair]
                    )
                )
        for copy in copies:
            copy.start()
        for copy in copies:
            copy.wait()

    return pl.pallas_call(
        kernel,
        grid_spec=pltpu.PrefetchScalarGridSpec(
            num_scalar_prefetch=1,
            grid=(1,),
            in_specs=[pl.BlockSpec(memory_space=pl.ANY)],
            out_specs=[pl.BlockSpec(memory_space=pl.ANY)] * len(sizes),
            scratch_shapes=[pltpu.SemaphoreType.DMA((half,))],
        ),
        out_shape=[jax.ShapeDtypeStruct((size, slot_rows, width), rows.dtype) for size in sizes],
        compiler_params=params(),
        name="gather_sent",
    )(scalars, rows)


def scatter_home(scalars, kept, back, half):
    slot_rows, width = kept.shape[1:]

    def kernel(scalars_ref, kept_ref, back_ref, out, sems):
        copies = []
        for i in range(half):
            copies.append(
                pltpu.make_async_copy(
                    kept_ref.at[i], out.at[kept_slot(scalars_ref, i, half)], sems.at[0, i]
                )
            )
            copies.append(
                pltpu.make_async_copy(
                    back_ref.at[i], out.at[sent_slot(scalars_ref, i, half)], sems.at[1, i]
                )
            )
        for copy in copies:
            copy.start()
        for copy in copies:
            copy.wait()

    return pl.pallas_call(
        kernel,
        grid_spec=pltpu.PrefetchScalarGridSpec(
            num_scalar_prefetch=1,
            grid=(1,),
            in_specs=[pl.BlockSpec(memory_space=pl.ANY)] * 2,
            out_specs=pl.BlockSpec(memory_space=pl.ANY),
            scratch_shapes=[pltpu.SemaphoreType.DMA((2, half))],
        ),
        out_shape=jax.ShapeDtypeStruct((2 * half, slot_rows, width), kept.dtype),
        compiler_params=params(),
        name="scatter_home",
    )(scalars, kept, back)


def split_heads(value):
    low = lax.broadcasted_iota(jnp.int32, value.shape, 1) < value.shape[1] // 2
    zero = jnp.zeros_like(value)
    return jnp.concatenate([jnp.where(low, value, zero), jnp.where(low, zero, value)], 0)


def side_by_side(value):
    rows = value.shape[0] // 2
    return jnp.concatenate([value[:rows], value[rows:]], 1)


def attention_forward(
    scalars, rows, received, live, w_qkv, b_qv, w_out, norm_gains, bias_rows, first, half
):
    slot_rows, width = rows.shape[1:]
    pairs = received.shape[0]
    length = 2 * slot_rows
    duo = 2 * width // HEADS
    blocks = width // duo
    score_scale = (width // HEADS) ** (-0.5)

    def kernel(
        scalars_ref,
        kept_a,
        kept_b,
        got,
        live_ref,
        w_qkv_ref,
        b_qv_ref,
        w_out_ref,
        gains_ref,
        biases_ref,
        joined_out,
        mixed_out,
        probs_out,
        context_out,
        normed_out,
        root_out,
        hidden_out,
    ):
        joined = jnp.concatenate([kept_a[0], got[0], kept_b[0], got[1]], 0)
        joined_out[...] = joined
        mixed = dot(joined, w_qkv_ref[...])
        queries = ((mixed[:, :width] + b_qv_ref[0:1, :]).astype(BF16).astype(F32) * score_scale).astype(BF16)
        keys = mixed[:, width : 2 * width].astype(BF16)
        values = (mixed[:, 2 * width :] + b_qv_ref[1:2, :]).astype(BF16)
        mixed_out[:, :width] = queries
        mixed_out[:, width : 2 * width] = keys
        mixed_out[:, 2 * width :] = values
        contexts = []
        for pair in range(2):
            seen = live_ref[pair] > 0
            span = slice(pair * length, (pair + 1) * length)
            heads = []
            for block in range(blocks):
                cols = slice(block * duo, (block + 1) * duo)
                scores = dot(split_heads(queries[span, cols]), keys[span, cols], 1, 1)
                scores = jnp.where(seen, scores, -1e30)
                powered = jnp.exp(scores - jnp.max(scores, axis=-1, keepdims=True))
                low_probs = (powered / jnp.sum(powered, axis=-1, keepdims=True)).astype(BF16)
                probs_out[pair, block] = low_probs
                heads.append(
                    dot(side_by_side(low_probs), split_heads(values[span, cols])).astype(BF16)
                )
            contexts.append(jnp.concatenate(heads, 1))
        context = jnp.concatenate(contexts, 0)
        context_out[...] = context
        pre_one = joined.astype(F32) + dot(context, w_out_ref[...]) + biases_ref[0:1, :]
        centered = pre_one - jnp.mean(pre_one, axis=-1, keepdims=True)
        root = lax.rsqrt(jnp.mean(centered * centered, axis=-1, keepdims=True) + EPSILON)
        normed = centered * root
        normed_out[...] = normed
        root_out[...] = jnp.broadcast_to(root, root_out.shape)
        hidden_out[...] = (normed * gains_ref[0:1, :] + biases_ref[1:2, :]).astype(BF16)

    def whole(array):
        return pl.BlockSpec(array.shape, lambda i, s: (0,) * array.ndim)

    def by_rows(columns):
        return pl.BlockSpec((2 * length, columns), lambda i, s: (i, 0))

    slot = (1, slot_rows, width)
    total = pairs * length
    return pl.pallas_call(
        kernel,
        grid_spec=pltpu.PrefetchScalarGridSpec(
            num_scalar_prefetch=1,
            grid=(pairs // 2,),
            in_specs=[
                pl.BlockSpec(slot, lambda i, s: (kept_slot(s, first + 2 * i, half), 0, 0)),
                pl.BlockSpec(slot, lambda i, s: (kept_slot(s, first + 2 * i + 1, half), 0, 0)),
                pl.BlockSpec((2, slot_rows, width), lambda i, s: (i, 0, 0)),
                pl.BlockSpec((2, 1, length), lambda i, s: (first // 2 + i, 0, 0)),
                whole(w_qkv),
                whole(b_qv),
                whole(w_out),
                whole(norm_gains),
                whole(bias_rows),
            ],
            out_specs=[
                by_rows(width),
                by_rows(3 * width),
                pl.BlockSpec((2, blocks, 2 * length, length), lambda i, s: (i, 0, 0, 0)),
                by_rows(width),
                by_rows(width),
                by_rows(128),
                by_rows(width),
            ],
        ),
        out_shape=[
            jax.ShapeDtypeStruct((total, width), BF16),
            jax.ShapeDtypeStruct((total, 3 * width), BF16),
            jax.ShapeDtypeStruct((pairs, blocks, 2 * length, length), BF16),
            jax.ShapeDtypeStruct((total, width), BF16),
            jax.ShapeDtypeStruct((total, width), F32),
            jax.ShapeDtypeStruct((total, 128), F32),
            jax.ShapeDtypeStruct((total, width), BF16),
        ],
        compiler_params=params(),
        cost_estimate=pl.CostEstimate(
            flops=2 * total * width * width * 5, bytes_accessed=20 * 2**20, transcendentals=0
        ),
        name="attention_forward",
    )(scalars, rows, rows, received, live, w_qkv, b_qv, w_out, norm_gains, bias_rows)


def row_sum(value):
    return jnp.sum(value, axis=0, keepdims=True)


def feed_forward(
    scalars, low_hidden, normed, cotangent, far_cot, w_in, b_in, w_back, norm_gains, bias_rows, half
):
    slot_rows, width = cotangent.shape[1:]
    total = normed.shape[0]
    inner_width = w_in.shape[1]
    length = 2 * slot_rows
    chunk = 768

    def kernel(
        scalars_ref,
        hidden_ref,
        normed_ref,
        cot_a,
        cot_b,
        cot_far,
        w_in_ref,
        b_in_ref,
        w_back_ref,
        gains_ref,
        biases_ref,
        act_out,
        slope_out,
        branch_out,
        d_two_out,
        kept_out,
        far_out,
        sums_out,
    ):
        @pl.when(pl.program_id(0) == 0)
        def _():
            sums_out[...] = jnp.zeros_like(sums_out)

        low_hidden = hidden_ref[...]
        pre_two = normed_ref[...] * gains_ref[0:1, :] + biases_ref[1:2, :] + biases_ref[2:3, :]
        for start in range(0, inner_width, chunk):
            cols = slice(start, start + chunk)
            inner = dot(low_hidden, w_in_ref[:, cols]) + b_in_ref[:, cols]
            normal = 0.5 + 0.5 * lax.erf(inner * (0.5**0.5))
            low_act = (inner * normal).astype(BF16)
            density = jnp.exp(inner * inner * -0.5) * 0.3989422804014327
            act_out[:, cols] = low_act
            slope_out[:, cols] = (normal + inner * density).astype(BF16)
            pre_two = pre_two + dot(low_act, w_back_ref[cols, :])
        centered = pre_two - jnp.mean(pre_two, axis=-1, keepdims=True)
        root = lax.rsqrt(jnp.mean(centered * centered, axis=-1, keepdims=True) + EPSILON)
        scaled = centered * root
        output = (scaled * gains_ref[1:2, :] + biases_ref[3:4, :]).astype(BF16)
        for i in range(2):
            kept_out[i] = output[i * length : i * length + slot_rows]
            far_out[i] = output[i * length + slot_rows : (i + 1) * length]
        cot = jnp.concatenate([cot_a[0], cot_far[0], cot_b[0], cot_far[1]], 0).astype(F32)
        lifted = cot * gains_ref[1:2, :]
        d_two = root * (
            lifted
            - jnp.mean(lifted, axis=-1, keepdims=True)
            - scaled * jnp.mean(lifted * scaled, axis=-1, keepdims=True)
        )
        d_two_out[...] = d_two
        branch_out[...] = d_two.astype(BF16)
        sums_out[0:1, :] += row_sum(cot * scaled)
        sums_out[1:2, :] += row_sum(cot)
        sums_out[2:3, :] += row_sum(d_two)

    def whole(array):
        return pl.BlockSpec(
            array.shape, lambda i, s: (0,) * array.ndim, pipeline_mode=pl.Buffered(1)
        )

    def by_rows(columns):
        return pl.BlockSpec((2 * length, columns), lambda i, s: (i, 0))

    slot = (1, slot_rows, width)
    duo = pl.BlockSpec((2, slot_rows, width), lambda i, s: (i, 0, 0))
    return pl.pallas_call(
        kernel,
        grid_spec=pltpu.PrefetchScalarGridSpec(
            num_scalar_prefetch=1,
            grid=(total // (2 * length),),
            in_specs=[
                by_rows(width),
                by_rows(width),
                pl.BlockSpec(slot, lambda i, s: (kept_slot(s, 2 * i, half), 0, 0)),
                pl.BlockSpec(slot, lambda i, s: (kept_slot(s, 2 * i + 1, half), 0, 0)),
                duo,
                whole(w_in),
                whole(b_in),
                whole(w_back),
                whole(norm_gains),
                whole(bias_rows),
            ],
            out_specs=[
                by_rows(inner_width),
                by_rows(inner_width),
                by_rows(width),
                by_rows(width),
                duo,
                duo,
                pl.BlockSpec((8, width), lambda i, s: (0, 0)),
            ],
        ),
        out_shape=[
            jax.ShapeDtypeStruct((total, inner_width), BF16),
            jax.ShapeDtypeStruct((total, inner_width), BF16),
            jax.ShapeDtypeStruct((total, width), BF16),
            jax.ShapeDtypeStruct((total, width), F32),
            jax.ShapeDtypeStruct((half, slot_rows, width), BF16),
            jax.ShapeDtypeStruct((half, slot_rows, width), BF16),
            jax.ShapeDtypeStruct((8, width), F32),
        ],
        compiler_params=params(),
        cost_estimate=pl.CostEstimate(
            flops=2 * total * width * inner_width * 4, bytes_accessed=30 * 2**20, transcendentals=0
        ),
        name="feed_forward",
    )(
        scalars,
        low_hidden,
        normed,
        cotangent,
        cotangent,
        far_cot,
        w_in,
        b_in,
        w_back,
        norm_gains,
        bias_rows,
    )


def feed_backward(branch, slope, d_two, normed, root, w_in, w_back, norm_gains):
    total, width = branch.shape
    inner_width = slope.shape[1]
    step = 256
    chunk = 768

    def kernel(
        branch_ref,
        slope_ref,
        d_two_ref,
        normed_ref,
        root_ref,
        w_in_ref,
        w_back_ref,
        gains_ref,
        low_inner_out,
        d_one_out,
        low_attn_out,
        sums_out,
        inner_sum_out,
    ):
        @pl.when(pl.program_id(0) == 0)
        def _():
            sums_out[...] = jnp.zeros_like(sums_out)
            inner_sum_out[...] = jnp.zeros_like(inner_sum_out)

        low_branch = branch_ref[...]
        d_hidden = d_two_ref[...]
        for start in range(0, inner_width, chunk):
            cols = slice(start, start + chunk)
            d_inner = dot(low_branch, w_back_ref[cols, :], 1, 1) * slope_ref[:, cols].astype(F32)
            low_inner = d_inner.astype(BF16)
            low_inner_out[:, cols] = low_inner
            inner_sum_out[0:1, cols] += row_sum(d_inner)
            d_hidden = d_hidden + dot(low_inner, w_in_ref[:, cols], 1, 1)
        normed = normed_ref[...]
        lifted = d_hidden * gains_ref[0:1, :]
        d_one = root_ref[:, 0:1] * (
            lifted
            - jnp.mean(lifted, axis=-1, keepdims=True)
            - normed * jnp.mean(lifted * normed, axis=-1, keepdims=True)
        )
        d_one_out[...] = d_one
        low_attn_out[...] = d_one.astype(BF16)
        sums_out[0:1, :] += row_sum(d_hidden * normed)
        sums_out[1:2, :] += row_sum(d_hidden)
        sums_out[2:3, :] += row_sum(d_one)

    def whole(array):
        return pl.BlockSpec(array.shape, lambda i: (0,) * array.ndim, pipeline_mode=pl.Buffered(1))

    def by_rows(columns):
        return pl.BlockSpec((step, columns), lambda i: (i, 0))

    return pl.pallas_call(
        kernel,
        grid=(total // step,),
        in_specs=[
            by_rows(width),
            by_rows(inner_width),
            by_rows(width),
            by_rows(width),
            by_rows(128),
            whole(w_in),
            whole(w_back),
            whole(norm_gains),
        ],
        out_specs=[
            by_rows(inner_width),
            by_rows(width),
            by_rows(width),
            pl.BlockSpec((8, width), lambda i: (0, 0)),
            pl.BlockSpec((8, inner_width), lambda i: (0, 0)),
        ],
        out_shape=[
            jax.ShapeDtypeStruct((total, inner_width), BF16),
            jax.ShapeDtypeStruct((total, width), F32),
            jax.ShapeDtypeStruct((total, width), BF16),
            jax.ShapeDtypeStruct((8, width), F32),
            jax.ShapeDtypeStruct((8, inner_width), F32),
        ],
        compiler_params=params(),
        cost_estimate=pl.CostEstimate(
            flops=2 * total * width * inner_width * 3, bytes_accessed=30 * 2**20, transcendentals=0
        ),
        name="feed_backward",
    )(branch, slope, d_two, normed, root, w_in, w_back, norm_gains)


def attention_backward(low_attn, mixed, probs, d_one, w_out, w_qkv):
    total, width = low_attn.shape
    pairs, blocks, _, length = probs.shape
    duo = width // blocks
    slot_rows = length // 2
    score_scale = (width // HEADS) ** (-0.5)

    def kernel(
        low_attn_ref,
        mixed_ref,
        probs_ref,
        d_one_ref,
        w_out_ref,
        w_qkv_ref,
        d_mixed_out,
        kept_out,
        far_out,
        sums_out,
    ):
        @pl.when(pl.program_id(0) == 0)
        def _():
            sums_out[...] = jnp.zeros_like(sums_out)

        d_context = dot(low_attn_ref[...], w_out_ref[...], 1, 1).astype(BF16)
        low = lax.broadcasted_iota(jnp.int32, (length, duo), 1) < duo // 2
        for pair in range(2):
            span = slice(pair * length, (pair + 1) * length)
            for block in range(blocks):
                cols = slice(block * duo, (block + 1) * duo)
                queries = split_heads(mixed_ref[span, cols])
                keys = mixed_ref[span, width + block * duo : width + (block + 1) * duo]
                values = mixed_ref[span, 2 * width + block * duo : 2 * width + (block + 1) * duo]
                d_heads = split_heads(d_context[span, cols])
                low_probs = probs_ref[pair, block]
                wide = low_probs.astype(F32)
                d_probs = dot(d_heads, values, 1, 1)
                d_scores = wide * (d_probs - jnp.sum(wide * d_probs, axis=-1, keepdims=True))
                d_scores = d_scores.astype(BF16)
                d_queries = dot(side_by_side(d_scores), split_heads(keys)) * score_scale
                d_mixed_out[span, cols] = d_queries.astype(BF16)
                d_mixed_out[span, width + block * duo : width + (block + 1) * duo] = dot(
                    d_scores, queries, 0, 0
                ).astype(BF16)
                d_mixed_out[span, 2 * width + block * duo : 2 * width + (block + 1) * duo] = dot(
                    low_probs, d_heads, 0, 0
                ).astype(BF16)
        d_mixed = d_mixed_out[...]
        sums_out[0:1, :] += row_sum(d_mixed[:, :width].astype(F32))
        sums_out[1:2, :] += row_sum(d_mixed[:, 2 * width :].astype(F32))
        d_rows = (d_one_ref[...] + dot(d_mixed, w_qkv_ref[...], 1, 1)).astype(BF16)
        for i in range(2):
            kept_out[i] = d_rows[i * length : i * length + slot_rows]
            far_out[i] = d_rows[i * length + slot_rows : (i + 1) * length]

    def whole(array):
        return pl.BlockSpec(array.shape, lambda i: (0,) * array.ndim, pipeline_mode=pl.Buffered(1))

    def by_rows(columns):
        return pl.BlockSpec((2 * length, columns), lambda i: (i, 0))

    two = pl.BlockSpec((2, slot_rows, width), lambda i: (i, 0, 0))
    return pl.pallas_call(
        kernel,
        grid=(pairs // 2,),
        in_specs=[
            by_rows(width),
            by_rows(3 * width),
            pl.BlockSpec((2, blocks, 2 * length, length), lambda i: (i, 0, 0, 0)),
            by_rows(width),
            whole(w_out),
            whole(w_qkv),
        ],
        out_specs=[by_rows(3 * width), two, two, pl.BlockSpec((8, width), lambda i: (0, 0))],
        out_shape=[
            jax.ShapeDtypeStruct((total, 3 * width), BF16),
            jax.ShapeDtypeStruct((pairs, slot_rows, width), BF16),
            jax.ShapeDtypeStruct((pairs, slot_rows, width), BF16),
            jax.ShapeDtypeStruct((8, width), F32),
        ],
        compiler_params=params(),
        cost_estimate=pl.CostEstimate(
            flops=2 * total * width * width * 10, bytes_accessed=20 * 2**20, transcendentals=0
        ),
        name="attention_backward",
    )(low_attn, mixed, probs, d_one, w_out, w_qkv)


def grad_by_columns(scalars, left, right, shards, chunk, base):
    total, height = left.shape
    width = right.shape[1]
    shard = height // shards
    places = shards // 2

    def kernel(scalars_ref, left_ref, right_ref, send_out, keep_out, held):
        core, place = scalars_ref[base + 1], scalars_ref[base + 2]
        held[...] = dot(left_ref[...], right_ref[...], 0, 0).astype(BF16)
        for j in range(places):
            row = (place ^ j) * 2
            send_out[j] = held[pl.ds(pl.multiple_of((row + 1 - core) * shard, 16), shard), :]
            keep_out[j] = held[pl.ds(pl.multiple_of((row + core) * shard, 16), shard), :]

    out = pl.BlockSpec((places, shard, chunk), lambda i, s: (0, 0, i))
    shape = jax.ShapeDtypeStruct((places, shard, width), BF16)
    return pl.pallas_call(
        kernel,
        grid_spec=pltpu.PrefetchScalarGridSpec(
            num_scalar_prefetch=1,
            grid=(width // chunk,),
            in_specs=[
                pl.BlockSpec((total, height), lambda i, s: (0, 0), pipeline_mode=pl.Buffered(1)),
                pl.BlockSpec((total, chunk), lambda i, s: (0, i)),
            ],
            out_specs=[out, out],
            scratch_shapes=[pltpu.VMEM((height, chunk), BF16)],
        ),
        out_shape=[shape, shape],
        compiler_params=params(),
        cost_estimate=pl.CostEstimate(
            flops=2 * total * width * height, bytes_accessed=12 * 2**20, transcendentals=0
        ),
        name="grad_by_columns",
    )(scalars, left, right)


def grad_by_rows(scalars, left, right, shards, base):
    total, height = left.shape
    width = right.shape[1]
    shard = height // shards
    places = shards // 2
    chunk = 4 * shard

    def kernel(scalars_ref, left_ref, right_ref, send_out, keep_out, held):
        core, place = scalars_ref[base + 1], scalars_ref[base + 2]
        held[...] = dot(left_ref[...], right_ref[...], 0, 0).astype(BF16)
        for j in range(2):
            row = ((place & 1) ^ j) * 2
            send_out[j] = held[pl.ds(pl.multiple_of((row + 1 - core) * shard, 16), shard), :]
            keep_out[j] = held[pl.ds(pl.multiple_of((row + core) * shard, 16), shard), :]

    out = pl.BlockSpec((2, shard, width), lambda i, s: ((s[base + 2] >> 1) ^ i, 0, 0))
    shape = jax.ShapeDtypeStruct((places, shard, width), BF16)
    return pl.pallas_call(
        kernel,
        grid_spec=pltpu.PrefetchScalarGridSpec(
            num_scalar_prefetch=1,
            grid=(height // chunk,),
            in_specs=[
                pl.BlockSpec((total, chunk), lambda i, s: (0, i)),
                pl.BlockSpec((total, width), lambda i, s: (0, 0), pipeline_mode=pl.Buffered(1)),
            ],
            out_specs=[out, out],
            scratch_shapes=[pltpu.VMEM((chunk, width), BF16)],
        ),
        out_shape=[shape, shape],
        compiler_params=params(),
        cost_estimate=pl.CostEstimate(
            flops=2 * total * width * height, bytes_accessed=12 * 2**20, transcendentals=0
        ),
        name="grad_by_rows",
    )(scalars, left, right)


def added(parts):
    total = parts[0].astype(F32)
    for part in parts[1:]:
        total = total + part.astype(F32)
    return total.astype(BF16)


def reduce_shards(send, keep, order):
    places, shard, width = send.shape
    bits = places.bit_length() - 1
    shape = (2,) * bits + (shard, width)
    held = [keep.reshape(shape), flipped(send, "dp", 1).reshape(shape)]
    left = list(range(bits))[::-1]
    for bit in order:
        dim = left.index(bit)
        away = added([lax.index_in_dim(part, 1, dim, keepdims=False) for part in held])
        held = [lax.index_in_dim(part, 0, dim, keepdims=False) for part in held]
        held.append(flipped(away, "dp", 2 << bit))
        left.remove(bit)
    mine = lax.optimization_barrier(added(held))
    return mine.astype(F32) + flipped(mine, "mod", 1).astype(F32)


def reduce_plain(left, right):
    share = lax.psum_scatter(dot(left, right, 0, 0), "dp", scatter_dimension=0, tiled=True)
    return lax.psum(share.astype(BF16), "mod").astype(F32)


def body(
    layer_rows,
    cotangent,
    row_live,
    partner,
    w_qkv,
    b_qv,
    w_out,
    norm_gains,
    bias_rows,
    w_in,
    b_in,
    w_back,
):
    side = lax.axis_index("mod")
    place = lax.axis_index("dp")
    shards = lax.axis_size("dp")
    groups = partner.shape[1]
    half = groups // 2
    width = layer_rows.shape[2]
    slot_rows = layer_rows.shape[1] // groups
    inner_width = w_in.shape[1]
    slots = (groups, slot_rows, width)
    rows = layer_rows[0].reshape(slots)
    cot = cotangent[0].reshape(slots)
    scalars = jnp.concatenate(
        [partner[0], jnp.stack([side, place & 1, place >> 1]).astype(jnp.int32)]
    )
    cut = half // 2
    sent_a, sent_b = gather_sent(scalars, rows, half, (0, cut, half))
    got_a = flipped(sent_a, "mod", 1)
    got_b = flipped(sent_b, "mod", 1)
    cot, got_b = lax.optimization_barrier((cot, got_b))
    (sent_cot,) = gather_sent(scalars, cot, half, (0, half))
    far_cot = flipped(sent_cot, "mod", 1)

    live = row_live.reshape(2, groups, slot_rows)
    words_live = lax.dynamic_slice_in_dim(live[0], side * half, half, 0)
    region_live = live[1][lax.dynamic_slice_in_dim(partner[0], side * half, half, 0)]
    is_first = side == 0
    seen = jnp.concatenate(
        [
            jnp.where(is_first, words_live, region_live),
            jnp.where(is_first, region_live, words_live),
        ],
        1,
    )[:, None, :]

    parts = [
        attention_forward(
            scalars, rows, got, seen, w_qkv, b_qv, w_out, norm_gains, bias_rows, first, half
        )
        for got, first in ((got_a, 0), (got_b, cut))
    ]
    joined, mixed, probs, context, normed, root, low_hidden = [
        jnp.concatenate([a, b], 0) for a, b in zip(*parts)
    ]
    b_in_row = b_in.reshape(1, inner_width)
    act, slope, branch, d_two, out_kept, out_far, sums_two = feed_forward(
        scalars,
        low_hidden,
        normed,
        cot,
        far_cot,
        w_in,
        b_in_row,
        w_back,
        norm_gains,
        bias_rows,
        half,
    )
    out_back = flipped(out_far, "mod", 1)
    low_inner, d_one, low_attn, sums_one, inner_sum = feed_backward(
        branch, slope, d_two, normed, root, w_in, w_back, norm_gains
    )
    d_mixed, d_kept, d_far, sums_qv = attention_backward(
        low_attn, mixed, probs, d_one, w_out, w_qkv
    )
    d_back = flipped(d_far, "mod", 1)

    aligned = shards % 4 == 0 and shards & (shards - 1) == 0 and (width // shards) % 16 == 0
    if aligned:
        bits = (shards // 2).bit_length() - 1
        order = list(range(bits))
        grad_back = reduce_shards(*grad_by_rows(scalars, act, branch, shards, groups), order)
        grad_in = reduce_shards(
            *grad_by_columns(scalars, low_hidden, low_inner, shards, 768, groups), order
        )
        grad_out = reduce_shards(
            *grad_by_columns(scalars, context, low_attn, shards, 768, groups), order
        )
        grad_qkv = reduce_shards(
            *grad_by_columns(scalars, joined, d_mixed, shards, 768, groups), order
        )
    else:
        grad_back = reduce_plain(act, branch)
        grad_in = reduce_plain(low_hidden, low_inner)
        grad_out = reduce_plain(context, low_attn)
        grad_qkv = reduce_plain(joined, d_mixed)

    small = jnp.concatenate(
        [
            sums_qv[0:2],
            sums_one[0:1],
            sums_two[0:1],
            sums_one[2:3],
            sums_one[1:2],
            sums_two[2:3],
            sums_two[1:2],
            inner_sum[0].reshape(-1, width),
        ],
        0,
    )
    small = lax.psum(small, ("mod", "dp"))
    shard = width // shards
    rows_small = lax.dynamic_slice_in_dim(small[:8], place * shard, shard, 1)
    inner_shard = inner_width // shards
    grad_b_in = lax.dynamic_slice_in_dim(small[8:].reshape(-1), place * inner_shard, inner_shard)

    out_rows = scatter_home(scalars, out_kept, out_back, half).reshape(1, -1, width)
    grad_rows = scatter_home(scalars, d_kept, d_back, half).reshape(1, -1, width)
    return (
        out_rows,
        grad_rows,
        grad_qkv,
        rows_small[0:2],
        grad_out,
        rows_small[2:4],
        rows_small[4:8],
        grad_in,
        grad_b_in,
        grad_back,
    )


def solution(mesh):
    return jax.shard_map(
        body,
        mesh=mesh,
        in_specs=(
            P("mod", "dp", None),
            P("mod", "dp", None),
            P(None, "dp"),
            P("dp", None),
            P(),
            P(),
            P(),
            P(),
            P(),
            P(),
            P(),
            P(),
        ),
        out_specs=(
            P("mod", "dp", None),
            P("mod", "dp", None),
            P("dp", None),
            P(None, "dp"),
            P("dp", None),
            P(None, "dp"),
            P(None, "dp"),
            P("dp", None),
            P("dp"),
            P("dp", None),
        ),
        check_vma=False,
    )
```

time: 923 us -> 513 us (0.56)
  waiting for transfers between devices: 423 us -> 117 us
  Pallas kernels: 0 us -> 275 us
  matrix products: 165 us -> 0 us
  local copies, waits for them, and re-layouts: 172 us -> 26.5 us
  other arithmetic: 64.9 us -> 21.3 us
  blocking collectives: 67.8 us -> 40 us
  starting transfers between devices: 5.01 us -> 31.2 us
  between operations: 15.8 us -> 1.07 us
    pallas_call x0 -> x13, Pallas kernels: none -> 275 us  [the longest x2 99.3 us: scatter_home(): pl.pallas_call(kernel, grid_spec=pltpu.PrefetchScalarGridSpec(num_scalar_...]
    reduce_scatter x3 -> x0, waiting for transfers between devices: 224 us -> none  [the longest x1 114 us: body(): lax.psum_scatter(grads[5], 'dp', scatter_dimension=0, tiled=True)]
    dot_general x18 -> x0, matrix products: 165 us -> none  [the longest x4 42.2 us: contract_cols(): lax.dot_general(left_side, right_side, (((1,), (1,)), ((), ())), preferre...]
    unnamed x1 -> x0, blocking collectives: 62.2 us -> none
    unnamed x12 -> x0, waiting for transfers between devices: 47.4 us -> none
    reshape x11 -> x1, local copies, waits for them, and re-layouts: 42.2 us -> 0.01 us  [body(): small[8:].reshape(-1)]
    psum x1 -> x0, waiting for transfers between devices: 37.2 us -> none  [body(): lax.psum(summed[0].astype(jnp.bfloat16), 'mod').astype(jnp.float32)]
    unnamed x109 -> x56, local copies, waits for them, and re-layouts: 45.3 us -> 10.1 us
  transfers between devices with their start and end apart: 10 -> 25, of which waited for: 6 -> 11; matrix products, arithmetic and copies ran while one was open for 21% -> 7% of each run, Pallas kernels for 0% -> 35%
where the time goes in v1:
time: 513 us; the launch traced here: 512 us
  Pallas kernels  275 us (54%)
  waiting for transfers between devices  117 us (23%)
  blocking collectives  40 us (8%)
  starting transfers between devices  31.2 us (6%)
  local copies, waits for them, and re-layouts  26.5 us (5%)
  other arithmetic  21.3 us (4%)
    ppermute x25, waiting for transfers between devices, flipped(): return lax.ppermute(value, axis, pairs)  117 us
    pallas_call x2, Pallas kernels, scatter_home(): pl.pallas_call(kernel, grid_spec=pltpu.PrefetchScalarGridSpec(num_scalar_...  99.3 us
    pallas_call x2, Pallas kernels, gather_sent(): pl.pallas_call(kernel, grid_spec=pltpu.PrefetchScalarGridSpec(num_scalar_...  51.5 us
    psum x1, blocking collectives, body(): small = lax.psum(small, ('mod', 'dp'))  40 us
    ppermute x25, starting transfers between devices, flipped(): return lax.ppermute(value, axis, pairs)  31.2 us
    pallas_call x1, Pallas kernels, attention_backward(): pl.pallas_call(kernel, grid=(pairs // 2,), in_specs=[by_rows(width), by_r...  27.6 us
    pallas_call x3, Pallas kernels, grad_by_columns(): pl.pallas_call(kernel, grid_spec=pltpu.PrefetchScalarGridSpec(num_scalar_...  24.5 us
    pallas_call x1, Pallas kernels, feed_forward(): pl.pallas_call(kernel, grid_spec=pltpu.PrefetchScalarGridSpec(num_scalar_...  22.5 us
  transfers between devices with their start and end apart: 25, of which 11 were waited for; matrix products, arithmetic and copies ran while one was open for 7% of the time, Pallas kernels for 35%

profile of v1, /device:TPU:0, one launch (start us, length us, event | category | flops | bytes accessed | tf_op | source)
XLA Modules:
  0.0 512.1 jit_solution(522895109829396242)
XLA Ops:
  2.0 25.7 %gather_sent.2 = (bf16[4,64,768]{2,1,0:T(8,128)(2,1)}, bf16[4,64,768]{2,1,0:T(8,128)(2,1)}) custom-call(s32[19]{0:T(128)} %pad_add_fusion.1.scalars_ref, bf16[16,64,768]{2,1,0:T(8,128)(2,1)} %bitcast.168), custom_call_target="tpu_custom_call" | custom-call | tf_op jit(solution)/shard_map/gather_sent/pallas_call | solution.py:66
  27.6 3.0 collective-permute-start.1
  32.2 8.6 %collective-permute-done.1.got = bf16[4,64,768]{2,1,0:T(8,128)(2,1)S(1)} collective-permute-done((bf16[4,64,768]{2,1,0:T(8,128)(2,1)}, bf16[4,64,768]{2,1,0:T(8,128)(2,1)S(1)}, u32[]{:S(2)}, u32[]{:S(2)}) %collective-permute-start.1) | collective-permute-done | bytes 393248 | tf_op jit(solution)/shard_map/ppermute | solution.py:25
  41.5 10.5 %attention_forward.3 = (bf16[512,768]{1,0:T(8,128)(2,1)}, bf16[512,2304]{1,0:T(8,128)(2,1)}, bf16[4,6,256,128]{3,2,1,0:T(8,128)(2,1)}, bf16[512,768]{1,0:T(8,128...) custom-call(s32[19]{0:T(128)} %pad_add_fusion.1.scalars_ref, ...), custom_call_target="tpu_custom_call" | custom-call | flops 3019898880 | bytes 20971520 | tf_op jit(solution)/shard_map/attention_forward/pallas_call | solution.py:200
  52.8 10.4 %attention_forward.2 = (bf16[512,768]{1,0:T(8,128)(2,1)}, bf16[512,2304]{1,0:T(8,128)(2,1)}, bf16[4,6,256,128]{3,2,1,0:T(8,128)(2,1)}, bf16[512,768]{1,0:T(8,128...) custom-call(s32[19]{0:T(128)} %pad_add_fusion.1.scalars_ref, ...), custom_call_target="tpu_custom_call" | custom-call | flops 3019898880 | bytes 20971520 | tf_op jit(solution)/shard_map/attention_forward/pallas_call | solution.py:200
  63.2 1.6 constant_dynamic-update-slice_fusion.3
  64.9 25.8 %gather_sent.3 = bf16[8,64,768]{2,1,0:T(8,128)(2,1)} custom-call(s32[19]{0:T(128)} %pad_add_fusion.1.scalars_ref, bf16[16,64,768]{2,1,0:T(8,128)(2,1)} %bitcast.173), custom_call_target="tpu_custom_call" | custom-call | tf_op jit(solution)/shard_map/gather_sent/pallas_call | solution.py:66
  90.7 2.1 collective-permute-start.2
  94.3 1.6 copy-done.7
  96.7 1.9 pad_maximum_fusion.1.probs_ref
  100.1 1.8 pad_maximum_fusion.2
  103.6 2.4 pad_maximum_fusion.mixed_ref
  106.0 2.9 collective-permute-done.2.cot_far
  109.8 22.5 %feed_forward.1 = (bf16[1024,3072]{1,0:T(8,128)(2,1)}, bf16[1024,3072]{1,0:T(8,128)(2,1)}, bf16[1024,768]{1,0:T(8,128)(2,1)}, f32[1024,768]{1,0:T(8,128)}, bf16[...) custom-call(s32[19]{0:T(128)} %pad_add_fusion.1.scalars_ref, bf16[1024,768]{1,0:T(8,128)(2,1)} %copy-done.16, ...), custom_call_target="tpu_custom_call" | custom-call | flops 19327352832 | bytes 31457280 | tf_op jit(solution)/shard_map/feed_forward/pallas_call | solution.py:321
  132.3 10.3 %grad_by_rows.1 = (bf16[8,192,768]{2,1,0:T(8,128)(2,1)}, bf16[8,192,768]{2,1,0:T(8,128)(2,1)}) custom-call(s32[19]{0:T(128)} %pad_add_fusion.1.scalars_ref, bf16[1024,3072]{1,0:T(8,128)(2,1)} %get-tuple-element.91.left_ref, bf16[1024,768]{1,0:T(8,128)(2,1)} %get-tuple-element.62.branch_ref.right_ref), custom_call_target="tpu_custom_call" | custom-call | flops 4831838208 | bytes 12582912 | tf_op jit(solution)/shard_map/grad_by_rows/pallas_call | solution.py:607
  142.6 18.7 %feed_backward.1 = (bf16[1024,3072]{1,0:T(8,128)(2,1)}, f32[1024,768]{1,0:T(8,128)}, bf16[1024,768]{1,0:T(8,128)(2,1)}, f32[8,768]{1,0:T(8,128)}, f32[8,3072]{1,0:T(8,128)}) custom-call(bf16[1024,768]{1,0:T(8,128)(2,1)} %get-tuple-element.62.branch_ref.right_ref, bf16[1024,3072]{1,0:T(8,128)(2,1)} %get-tuple-element.63.slope_ref, ...), custom_call_target="tpu_custom_call" | custom-call | flops 14495514624 | bytes 31457280 | tf_op jit(solution)/shard_map/feed_backward/pallas_call | solution.py:431
  161.2 10.5 %grad_by_columns.5 = (bf16[8,48,3072]{2,1,0:T(8,128)(2,1)}, bf16[8,48,3072]{2,1,0:T(8,128)(2,1)}) custom-call(s32[19]{0:T(128)} %pad_add_fusion.1.scalars_ref, bf16[1024,768]{1,0:T(8,128)(2,1)} %copy-done.16, bf16[1024,3072]{1,0:T(8,128)(2,1)} %get-tuple-element.88.right_ref), custom_call_target="tpu_custom_call" | custom-call | flops 4831838208 | bytes 12582912 | tf_op jit(solution)/shard_map/grad_by_columns/pallas_call | solution.py:569
  173.1 5.0 grad_by_columns.4
  180.5 1.4 fusion.22
  181.9 27.6 %attention_backward.1 = (bf16[1024,2304]{1,0:T(8,128)(2,1)}, bf16[8,64,768]{2,1,0:T(8,128)(2,1)}, bf16[8,64,768]{2,1,0:T(8,128)(2,1)}, f32[8,768]{1,0:T(8,128)}) custom-call(bf16[1024,768]{1,0:T(8,128)(2,1)} %get-tuple-element.67.low_attn_ref.right_ref, bf16[1024,2304]{1,0:T(8,128)(2,1)} %pad_maximum_fusion.mixed_ref, ...), custom_call_target="tpu_custom_call" | custom-call | flops 12079595520 | bytes 20971520 | tf_op jit(solution)/shard_map/attention_backward/pallas_call | solution.py:527
  209.6 8.9 %grad_by_columns.3 = (bf16[8,48,2304]{2,1,0:T(8,128)(2,1)}, bf16[8,48,2304]{2,1,0:T(8,128)(2,1)}) custom-call(s32[19]{0:T(128)} %pad_add_fusion.1.scalars_ref, bf16[1024,768]{1,0:T(8,128)(2,1)} %get-tuple-element.106.left_ref, bf16[1024,2304]{1,0:T(8,128)(2,1)} %get-tuple-element.77.right_ref), custom_call_target="tpu_custom_call" | custom-call | flops 3623878656 | bytes 12582912 | tf_op jit(solution)/shard_map/grad_by_columns/pallas_call | solution.py:569
  220.6 1.5 collective-permute-start.11
  224.5 40.0 %psum.7 = f32[12,768]{1,0:T(8,128)S(1)} all-reduce(f32[12,768]{1,0:T(8,128)S(1)} %concatenate.38), channel_id=1, replica_groups=mesh['mod'=2,'dp'=16] {'mod','dp'}, use_global_device_ids=true, to_apply=%region_0.1 | all-reduce | flops 9216 | bytes 73728 | tf_op jit(solution)/shard_map/psum | solution.py:769
  264.6 2.3 collective-permute-start.4
  267.1 1.7 collective-permute-start.12
  270.2 2.8 collective-permute-done.12
  273.1 2.5 collective-permute-start.13
  275.6 3.0 collective-permute-done.13
  279.3 6.3 %collective-permute-done.4.back_ref = bf16[8,64,768]{2,1,0:T(8,128)(2,1)} collective-permute-done((bf16[8,64,768]{2,1,0:T(8,128)(2,1)}, bf16[8,64,768]{2,1,0:T(8,128)(2,1)}, u32[]{:S(2)}, u32[]{:S(2)}) %collective-permute-start.4) | collective-permute-done | bytes 786464 | tf_op jit(solution)/shard_map/ppermute | solution.py:25
  285.6 1.9 collective-permute-start.14
  289.3 49.6 %scatter_home.3 = bf16[16,64,768]{2,1,0:T(8,128)(2,1)} custom-call(s32[19]{0:T(128)} %pad_add_fusion.1.scalars_ref, bf16[8,64,768]{2,1,0:T(8,128)(2,1)} %get-tuple-element.73.kept_ref, bf16[8,64,768]{2,1,0:T(8,128)(2,1)} %collective-permute-done.4.back_ref), custom_call_target="tpu_custom_call" | custom-call | tf_op jit(solution)/shard_map/scatter_home/pallas_call | solution.py:102
  338.9 49.7 %scatter_home.2 = bf16[16,64,768]{2,1,0:T(8,128)(2,1)} custom-call(s32[19]{0:T(128)} %pad_add_fusion.1.scalars_ref, bf16[8,64,768]{2,1,0:T(8,128)(2,1)} %get-tuple-element.60.kept_ref, bf16[8,64,768]{2,1,0:T(8,128)(2,1)} %collective-permute-done.3.back_ref), custom_call_target="tpu_custom_call" | custom-call | tf_op jit(solution)/shard_map/scatter_home/pallas_call | solution.py:102
  388.7 1.6 convert_add_fusion.11
  390.2 1.5 fusion.2
  391.8 1.6 collective-permute-start.6
  394.7 1.7 fusion.1
  396.9 1.7 fusion
  400.0 1.6 collective-permute-start.16
  402.9 11.5 %collective-permute-done.6 = bf16[2,2,48,2304]{3,2,1,0:T(8,128)(2,1)S(1)} collective-permute-done((bf16[2,2,48,2304]{3,2,1,0:T(8,128)(2,1)S(1)}, bf16[2,2,48,2304]{3,2,1,0:T(8,128)(2,1)S(1)}, u32[]{:S(2)}, u32[]{:S(2)}) %collective-permute-start.6) | collective-permute-done | bytes 884768 | tf_op jit(solution)/shard_map/ppermute | solution.py:25
  414.6 1.7 collective-permute-start.7
  416.3 23.4 %collective-permute-done.21 = bf16[2,2,192,768]{3,2,1,0:T(8,128)(2,1)S(1)} collective-permute-done((bf16[2,2,192,768]{3,2,1,0:T(8,128)(2,1)S(1)}, bf16[2,2,192,768]{3,2,1,0:T(8,128)(2,1)S(1)}, u32[]{:S(2)}, u32[]{:S(2)}) %collective-permute-start.21) | collective-permute-done | bytes 1179680 | tf_op jit(solution)/shard_map/ppermute | solution.py:25
  439.9 1.7 collective-permute-start.22
  441.6 21.2 %collective-permute-done.16 = bf16[2,2,48,3072]{3,2,1,0:T(8,128)(2,1)S(1)} collective-permute-done((bf16[2,2,48,3072]{3,2,1,0:T(8,128)(2,1)S(1)}, bf16[2,2,48,3072]{3,2,1,0:T(8,128)(2,1)S(1)}, u32[]{:S(2)}, u32[]{:S(2)}) %collective-permute-start.16) | collective-permute-done | bytes 1179680 | tf_op jit(solution)/shard_map/ppermute | solution.py:25
  463.1 1.7 collective-permute-start.17
  466.4 1.8 collective-permute-start.23
  468.1 19.3 %collective-permute-done.17 = bf16[2,48,3072]{2,1,0:T(8,128)(2,1)S(1)} collective-permute-done((bf16[2,48,3072]{2,1,0:T(8,128)(2,1)S(1)}, bf16[2,48,3072]{2,1,0:T(8,128)(2,1)S(1)}, u32[]{:S(2)}, u32[]{:S(2)}) %collective-permute-start.17) | collective-permute-done | bytes 589856 | tf_op jit(solution)/shard_map/ppermute | solution.py:25
  490.6 11.4 %collective-permute-done.18 = bf16[48,3072]{1,0:T(8,128)(2,1)S(1)} collective-permute-done((bf16[48,3072]{1,0:T(8,128)(2,1)S(1)}, bf16[48,3072]{1,0:T(8,128)(2,1)S(1)}, u32[]{:S(2)}, u32[]{:S(2)}) %collective-permute-start.18) | collective-permute-done | bytes 294944 | tf_op jit(solution)/shard_map/ppermute | solution.py:25
  504.8 6.4 %collective-permute-done.19 = bf16[48,3072]{1,0:T(8,128)(2,1)S(1)} collective-permute-done((bf16[48,3072]{1,0:T(8,128)(2,1)S(1)}, bf16[48,3072]{1,0:T(8,128)(2,1)S(1)}, u32[]{:S(2)}, u32[]{:S(2)}) %collective-permute-start.19) | collective-permute-done | bytes 294944 | tf_op jit(solution)/shard_map/ppermute | solution.py:25
  (130 shorter events, 36.5 us)
Async XLA Ops:
  0.6 30.1 %copy-start.23 = (s32[1,16]{1,0:T(1,128)S(1)}, s32[1,16]{1,0:T(1,128)}, u32[]{:S(2)}) copy-start(s32[1,16]{1,0:T(1,128)} %param.15) | copy-start | bytes 196
  0.7 30.2 %copy-start.22 = (s32[2,1024]{1,0:T(2,128)S(1)}, s32[2,1024]{1,0:T(2,128)}, u32[]{:S(2)}) copy-start(s32[2,1024]{1,0:T(2,128)} %param.14) | copy-start | bytes 24580
  27.6 13.2 %collective-permute-start.1 = (bf16[4,64,768]{2,1,0:T(8,128)(2,1)}, bf16[4,64,768]{2,1,0:T(8,128)(2,1)S(1)}, u32[]{:S(2)}, u32[]{:S(2)}) collective-permute-start(bf16[4,64,768]{2,1,0:T(8,128)(2,1)} %get-tuple-element.54), channel_id=1, source_target_pairs={{0,16},{16,0},{1,17},{17,1},{2,18},{18,2},{3,19},{19,3},{4,20},{20... | collective-permute-start | bytes 1179656 | tf_op jit(solution)/shard_map/ppermute | solution.py:25
  30.7 21.4 %collective-permute-start = (bf16[4,64,768]{2,1,0:T(8,128)(2,1)}, bf16[4,64,768]{2,1,0:T(8,128)(2,1)S(1)}, u32[]{:S(2)}, u32[]{:S(2)}) collective-permute-start(bf16[4,64,768]{2,1,0:T(8,128)(2,1)} %get-tuple-element.52), channel_id=1, source_target_pairs={{0,16},{16,0},{1,17},{17,1},{2,18},{18,2},{3,19},{19,3},{4,20},{20... | collective-permute-start | bytes 1179656 | tf_op jit(solution)/shard_map/ppermute | solution.py:25
  63.2 1.6 copy-start.14
  64.9 27.9 %copy-start.5 = (f32[512,768]{1,0:T(8,128)S(1)}, f32[512,768]{1,0:T(8,128)}, u32[]{:S(2)}) copy-start(f32[512,768]{1,0:T(8,128)} %get-tuple-element.58) | copy-start | bytes 4718596
  90.7 18.2 %collective-permute-start.2 = (bf16[8,64,768]{2,1,0:T(8,128)(2,1)}, bf16[8,64,768]{2,1,0:T(8,128)(2,1)S(1)}, u32[]{:S(2)}, u32[]{:S(2)}) collective-permute-start(bf16[8,64,768]{2,1,0:T(8,128)(2,1)} %gather_sent.3), channel_id=1, source_target_pairs={{0,16},{16,0},{1,17},{17,1},{2,18},{18,2},{3,19},{19,3},{4,20},{20... | collective-permute-start | bytes 2359304 | tf_op jit(solution)/shard_map/ppermute | solution.py:25
  92.8 3.1 copy-start.7
  92.9 5.6 %copy-start.12 = (f32[1024,768]{1,0:T(8,128)}, f32[1024,768]{1,0:T(8,128)S(1)}, u32[]{:S(2)}) copy-start(f32[1024,768]{1,0:T(8,128)S(1)} %constant_dynamic-update-slice_fusion.2.normed_ref) | copy-start | bytes 9437188
  93.0 3.7 copy-start.6
  94.3 4.3 copy-start.16
  96.7 1.9 copy-start.19
  96.7 1.9 copy-start.20
  96.7 2.8 copy-start.9
  96.7 2.8 copy-start.10
  96.7 2.9 copy-start.11
  100.1 2.8 copy-start.2
  100.1 3.5 copy-start.3
  142.6 252.1 %collective-permute-start.20 = (bf16[8,192,768]{2,1,0:T(8,128)(2,1)}, bf16[8,192,768]{2,1,0:T(8,128)(2,1)}, u32[]{:S(2)}, u32[]{:S(2)}) collective-permute-start(bf16[8,192,768]{2,1,0:T(8,128)(2,1)} %get-tuple-element.93), channel_id=1, source_target_pairs={{0,1},{1,0},{2,3},{3,2},{4,5},{5,4},{6,7},{7,6},{8,9},{9,8},{10,11... | collective-permute-start | bytes 7077896 | tf_op jit(solution)/shard_map/ppermute | solution.py:25
  178.1 41.6 %collective-permute-start.10 = (bf16[8,48,768]{2,1,0:T(8,128)(2,1)}, bf16[8,48,768]{2,1,0:T(8,128)(2,1)S(1)}, u32[]{:S(2)}, u32[]{:S(2)}) collective-permute-start(bf16[8,48,768]{2,1,0:T(8,128)(2,1)} %get-tuple-element.87), channel_id=1, source_target_pairs={{0,1},{1,0},{2,3},{3,2},{4,5},{5,4},{6,7},{7,6},{8,9},{9,8},{10,11... | collective-permute-start | bytes 1769480 | tf_op jit(solution)/shard_map/ppermute | solution.py:25
  220.6 46.4 %collective-permute-start.11 = (bf16[2,2,48,768]{3,2,1,0:T(8,128)(2,1)}, bf16[2,2,48,768]{3,2,1,0:T(8,128)(2,1)S(1)}, u32[]{:S(2)}, u32[]{:S(2)}) collective-permute-start(bf16[2,2,48,768]{3,2,1,0:T(8,128)(2,1)} %fusion.15), channel_id=1, source_target_pairs={{0,2},{1,3},{2,0},{3,1},{4,6},{5,7},{6,4},{7,5},{8,10},{9,11},{10,... | collective-permute-start | bytes 884744 | tf_op jit(solution)/shard_map/ppermute | solution.py:25
  264.5 4.3 copy-start.21
  264.5 125.7 %collective-permute-start.5 = (bf16[8,48,2304]{2,1,0:T(8,128)(2,1)}, bf16[8,48,2304]{2,1,0:T(8,128)(2,1)}, u32[]{:S(2)}, u32[]{:S(2)}) collective-permute-start(bf16[8,48,2304]{2,1,0:T(8,128)(2,1)} %get-tuple-element.79), channel_id=1, source_target_pairs={{0,1},{1,0},{2,3},{3,2},{4,5},{5,4},{6,7},{7,6},{8,9},{9,8},{10,11... | collective-permute-start | bytes 5308424 | tf_op jit(solution)/shard_map/ppermute | solution.py:25
  264.6 21.0 %collective-permute-start.4 = (bf16[8,64,768]{2,1,0:T(8,128)(2,1)}, bf16[8,64,768]{2,1,0:T(8,128)(2,1)}, u32[]{:S(2)}, u32[]{:S(2)}) collective-permute-start(bf16[8,64,768]{2,1,0:T(8,128)(2,1)} %get-tuple-element.74), channel_id=1, source_target_pairs={{0,16},{16,0},{1,17},{17,1},{2,18},{18,2},{3,19},{19,3},{4,20},{20... | collective-permute-start | bytes 2359304 | tf_op jit(solution)/shard_map/ppermute | solution.py:25
  266.9 72.0 %collective-permute-start.3 = (bf16[8,64,768]{2,1,0:T(8,128)(2,1)}, bf16[8,64,768]{2,1,0:T(8,128)(2,1)}, u32[]{:S(2)}, u32[]{:S(2)}) collective-permute-start(bf16[8,64,768]{2,1,0:T(8,128)(2,1)} %get-tuple-element.61), channel_id=1, source_target_pairs={{0,16},{16,0},{1,17},{17,1},{2,18},{18,2},{3,19},{19,3},{4,20},{20... | collective-permute-start | bytes 2359304 | tf_op jit(solution)/shard_map/ppermute | solution.py:25
  267.0 1.8 copy-start.17
  267.1 5.9 %collective-permute-start.12 = (bf16[2,48,768]{2,1,0:T(8,128)(2,1)S(1)}, bf16[2,48,768]{2,1,0:T(8,128)(2,1)S(1)}, u32[]{:S(2)}, u32[]{:S(2)}) collective-permute-start(bf16[2,48,768]{2,1,0:T(8,128)(2,1)S(1)} %fusion.16), channel_id=1, source_target_pairs={{0,4},{1,5},{2,6},{3,7},{4,0},{5,1},{6,2},{7,3},{8,12},{9,13},{10,... | collective-permute-start | bytes 442376 | tf_op jit(solution)/shard_map/ppermute | solution.py:25
  268.8 4.2 copy-start.18
  268.8 6.8 %slice-start = ((f32[12,768]{1,0:T(8,128)}), f32[8,768]{1,0:T(8,128)S(1)}, s32[]{:S(2)}) async-start(f32[12,768]{1,0:T(8,128)} %copy-done.21), calls=%async_computation | async-start | bytes 49152 | tf_op jit(solution)/shard_map/slice | solution.py:771
  268.8 19.9 %slice-start.1 = ((f32[12,768]{1,0:T(8,128)}), f32[4,768]{1,0:T(4,128)S(1)}, s32[]{:S(2)}) async-start(f32[12,768]{1,0:T(8,128)} %copy-done.21), calls=%async_computation.1 | async-start | bytes 24576 | tf_op jit(solution)/shard_map/slice | solution.py:773
  273.1 5.6 %collective-permute-start.13 = (bf16[48,768]{1,0:T(8,128)(2,1)S(1)}, bf16[48,768]{1,0:T(8,128)(2,1)S(1)}, u32[]{:S(2)}, u32[]{:S(2)}) collective-permute-start(bf16[48,768]{1,0:T(8,128)(2,1)S(1)} %fusion.17), channel_id=1, source_target_pairs={{0,8},{1,9},{2,10},{3,11},{4,12},{5,13},{6,14},{7,15},{8,0},{9,1},... | collective-permute-start | bytes 221192 | tf_op jit(solution)/shard_map/ppermute | solution.py:25
  278.6 118.3 %collective-permute-start.15 = (bf16[8,48,3072]{2,1,0:T(8,128)(2,1)}, bf16[8,48,3072]{2,1,0:T(8,128)(2,1)}, u32[]{:S(2)}, u32[]{:S(2)}) collective-permute-start(bf16[8,48,3072]{2,1,0:T(8,128)(2,1)} %get-tuple-element.90), channel_id=1, source_target_pairs={{0,1},{1,0},{2,3},{3,2},{4,5},{5,4},{6,7},{7,6},{8,9},{9,8},{10,11... | collective-permute-start | bytes 7077896 | tf_op jit(solution)/shard_map/ppermute | solution.py:25
  285.6 103.1 %collective-permute-start.14 = (bf16[48,768]{1,0:T(8,128)(2,1)}, bf16[48,768]{1,0:T(8,128)(2,1)S(1)}, u32[]{:S(2)}, u32[]{:S(2)}) collective-permute-start(bf16[48,768]{1,0:T(8,128)(2,1)} %fusion.19), channel_id=1, source_target_pairs={{0,16},{16,0},{1,17},{17,1},{2,18},{18,2},{3,19},{19,3},{4,20},{20... | collective-permute-start | bytes 221192 | tf_op jit(solution)/shard_map/ppermute | solution.py:25
  338.9 51.3 %copy-start.4 = (bf16[8,48,2304]{2,1,0:T(8,128)(2,1)S(1)}, bf16[8,48,2304]{2,1,0:T(8,128)(2,1)}, u32[]{:S(2)}) copy-start(bf16[8,48,2304]{2,1,0:T(8,128)(2,1)} %get-tuple-element.78) | copy-start | bytes 5308420
  390.2 4.4 copy-start
  391.8 22.6 %collective-permute-start.6 = (bf16[2,2,48,2304]{3,2,1,0:T(8,128)(2,1)S(1)}, bf16[2,2,48,2304]{3,2,1,0:T(8,128)(2,1)S(1)}, u32[]{:S(2)}, u32[]{:S(2)}) collective-permute-start(bf16[2,2,48,2304]{3,2,1,0:T(8,128)(2,1)S(1)} %fusion.2), channel_id=1, source_target_pairs={{0,2},{1,3},{2,0},{3,1},{4,6},{5,7},{6,4},{7,5},{8,10},{9,11},{10,... | collective-permute-start | bytes 2654216 | tf_op jit(solution)/shard_map/ppermute | solution.py:25
  394.6 2.3 copy-start.1
  396.4 43.3 %collective-permute-start.21 = (bf16[2,2,192,768]{3,2,1,0:T(8,128)(2,1)S(1)}, bf16[2,2,192,768]{3,2,1,0:T(8,128)(2,1)S(1)}, u32[]{:S(2)}, u32[]{:S(2)}) collective-permute-start(bf16[2,2,192,768]{3,2,1,0:T(8,128)(2,1)S(1)} %fusion.1), channel_id=1, source_target_pairs={{0,2},{1,3},{2,0},{3,1},{4,6},{5,7},{6,4},{7,5},{8,10},{9,11},{10,... | collective-permute-start | bytes 3538952 | tf_op jit(solution)/shard_map/ppermute | solution.py:25
  400.0 62.9 %collective-permute-start.16 = (bf16[2,2,48,3072]{3,2,1,0:T(8,128)(2,1)S(1)}, bf16[2,2,48,3072]{3,2,1,0:T(8,128)(2,1)S(1)}, u32[]{:S(2)}, u32[]{:S(2)}) collective-permute-start(bf16[2,2,48,3072]{3,2,1,0:T(8,128)(2,1)S(1)} %fusion), channel_id=1, source_target_pairs={{0,2},{1,3},{2,0},{3,1},{4,6},{5,7},{6,4},{7,5},{8,10},{9,11},{10,... | collective-permute-start | bytes 3538952 | tf_op jit(solution)/shard_map/ppermute | solution.py:25
  414.6 50.2 %collective-permute-start.7 = (bf16[2,48,2304]{2,1,0:T(8,128)(2,1)S(1)}, bf16[2,48,2304]{2,1,0:T(8,128)(2,1)S(1)}, u32[]{:S(2)}, u32[]{:S(2)}) collective-permute-start(bf16[2,48,2304]{2,1,0:T(8,128)(2,1)S(1)} %fusion.11), channel_id=1, source_target_pairs={{0,4},{1,5},{2,6},{3,7},{4,0},{5,1},{6,2},{7,3},{8,12},{9,13},{10,... | collective-permute-start | bytes 1327112 | tf_op jit(solution)/shard_map/ppermute | solution.py:25
  439.9 26.3 %collective-permute-start.22 = (bf16[2,192,768]{2,1,0:T(8,128)(2,1)S(1)}, bf16[2,192,768]{2,1,0:T(8,128)(2,1)S(1)}, u32[]{:S(2)}, u32[]{:S(2)}) collective-permute-start(bf16[2,192,768]{2,1,0:T(8,128)(2,1)S(1)} %fusion.4), channel_id=1, source_target_pairs={{0,4},{1,5},{2,6},{3,7},{4,0},{5,1},{6,2},{7,3},{8,12},{9,13},{10,... | collective-permute-start | bytes 1769480 | tf_op jit(solution)/shard_map/ppermute | solution.py:25
  463.1 24.4 %collective-permute-start.17 = (bf16[2,48,3072]{2,1,0:T(8,128)(2,1)S(1)}, bf16[2,48,3072]{2,1,0:T(8,128)(2,1)S(1)}, u32[]{:S(2)}, u32[]{:S(2)}) collective-permute-start(bf16[2,48,3072]{2,1,0:T(8,128)(2,1)S(1)} %fusion.3), channel_id=1, source_target_pairs={{0,4},{1,5},{2,6},{3,7},{4,0},{5,1},{6,2},{7,3},{8,12},{9,13},{10,... | collective-permute-start | bytes 1769480 | tf_op jit(solution)/shard_map/ppermute | solution.py:25
  464.9 23.1 %collective-permute-start.8 = (bf16[48,2304]{1,0:T(8,128)(2,1)S(1)}, bf16[48,2304]{1,0:T(8,128)(2,1)S(1)}, u32[]{:S(2)}, u32[]{:S(2)}) collective-permute-start(bf16[48,2304]{1,0:T(8,128)(2,1)S(1)} %fusion.12), channel_id=1, source_target_pairs={{0,8},{1,9},{2,10},{3,11},{4,12},{5,13},{6,14},{7,15},{8,0},{9,1},... | collective-permute-start | bytes 663560 | tf_op jit(solution)/shard_map/ppermute | solution.py:25
  466.4 22.8 %collective-permute-start.23 = (bf16[192,768]{1,0:T(8,128)(2,1)S(1)}, bf16[192,768]{1,0:T(8,128)(2,1)S(1)}, u32[]{:S(2)}, u32[]{:S(2)}) collective-permute-start(bf16[192,768]{1,0:T(8,128)(2,1)S(1)} %fusion.5), channel_id=1, source_target_pairs={{0,8},{1,9},{2,10},{3,11},{4,12},{5,13},{6,14},{7,15},{8,0},{9,1},... | collective-permute-start | bytes 884744 | tf_op jit(solution)/shard_map/ppermute | solution.py:25
  487.6 14.4 %collective-permute-start.18 = (bf16[48,3072]{1,0:T(8,128)(2,1)S(1)}, bf16[48,3072]{1,0:T(8,128)(2,1)S(1)}, u32[]{:S(2)}, u32[]{:S(2)}) collective-permute-start(bf16[48,3072]{1,0:T(8,128)(2,1)S(1)} %fusion.8), channel_id=1, source_target_pairs={{0,8},{1,9},{2,10},{3,11},{4,12},{5,13},{6,14},{7,15},{8,0},{9,1},... | collective-permute-start | bytes 884744 | tf_op jit(solution)/shard_map/ppermute | solution.py:25
  488.2 14.9 %collective-permute-start.9 = (bf16[48,2304]{1,0:T(8,128)(2,1)S(1)}, bf16[48,2304]{1,0:T(8,128)(2,1)S(1)}, u32[]{:S(2)}, u32[]{:S(2)}) collective-permute-start(bf16[48,2304]{1,0:T(8,128)(2,1)S(1)} %fusion.14), channel_id=1, source_target_pairs={{0,16},{16,0},{1,17},{17,1},{2,18},{18,2},{3,19},{19,3},{4,20},{20... | collective-permute-start | bytes 663560 | tf_op jit(solution)/shard_map/ppermute | solution.py:25
  489.3 14.6 %collective-permute-start.24 = (bf16[192,768]{1,0:T(8,128)(2,1)S(1)}, bf16[192,768]{1,0:T(8,128)(2,1)S(1)}, u32[]{:S(2)}, u32[]{:S(2)}) collective-permute-start(bf16[192,768]{1,0:T(8,128)(2,1)S(1)} %fusion.7), channel_id=1, source_target_pairs={{0,16},{16,0},{1,17},{17,1},{2,18},{18,2},{3,19},{19,3},{4,20},{20... | collective-permute-start | bytes 884744 | tf_op jit(solution)/shard_map/ppermute | solution.py:25
  502.2 9.0 %collective-permute-start.19 = (bf16[48,3072]{1,0:T(8,128)(2,1)S(1)}, bf16[48,3072]{1,0:T(8,128)(2,1)S(1)}, u32[]{:S(2)}, u32[]{:S(2)}) collective-permute-start(bf16[48,3072]{1,0:T(8,128)(2,1)S(1)} %fusion.10), channel_id=1, source_target_pairs={{0,16},{16,0},{1,17},{17,1},{2,18},{18,2},{3,19},{19,3},{4,20},{20... | collective-permute-start | bytes 884744 | tf_op jit(solution)/shard_map/ppermute | solution.py:25
  (6 other events, 6.6 us)
